TPU v7x, 32 devices: a whole 2x2x4 slice. The times are simulated.
32 devices in a mesh: dp: 8 (over z, x), tensor: 4 (over y, core).
Axes of the slice: x: 2, y: 2, z: 4, core: 2. Of those that a mesh axis runs over, the one named last changes fastest.
Arguments:
- activations: bfloat16 [2048, 768], P('dp', 'tensor'), may hold values from -6 to 6
- output_grad: bfloat16 [2048, 768], P('dp', 'tensor'), may hold values from -6 to 6
- seq_lengths: int32 [16], P('dp'), may hold values from 0 to 256, as said below
- routes: int32 [2048, 1], P('dp'), may hold values from 0 to 7; in each aligned block of 256 rows (0 to 255, 256 to 511, ...) at most 36 rows name the same one
- buckets: int32 [256], replicated, may hold values from 0 to 31
- norm1_gain: bfloat16 [768], P('tensor'), may hold values from 0.5 to 1.5
- w_query: bfloat16 [768, 768], P(None, 'tensor'), may hold values from -0.21875 to 0.21875
- w_key: bfloat16 [768, 768], P(None, 'tensor'), may hold values from -0.21875 to 0.21875
- w_value: bfloat16 [768, 768], P(None, 'tensor'), may hold values from -0.21875 to 0.21875
- w_output: bfloat16 [768, 768], P('tensor'), may hold values from -1.25 to 1.25
- bias_table: bfloat16 [32, 12], P(None, 'tensor'), may hold values from -4 to 4
- norm2_gain: bfloat16 [768], replicated, may hold values from 0.5 to 1.5
- w_router: bfloat16 [768, 8], replicated, may hold values from -0.15625 to 0.15625
- w_in: bfloat16 [8, 768, 3072], P('dp', None, 'tensor'), may hold values from -0.21875 to 0.21875
- w_out: bfloat16 [8, 3072, 768], P('dp', 'tensor'), may hold values from -1.25 to 1.25
Outputs:
- block_output: bfloat16 [2048, 768], P('dp', 'tensor')
- input_grad: float32 [2048, 768], P('dp', 'tensor')
- grad_norm1_gain: float32 [768], P('tensor')
- grad_w_query: float32 [768, 768], P(None, 'tensor')
- grad_w_key: float32 [768, 768], P(None, 'tensor')
- grad_w_value: float32 [768, 768], P(None, 'tensor')
- grad_w_output: float32 [768, 768], P('tensor')
- grad_bias_table: float32 [32, 12], P(None, 'tensor')
- grad_norm2_gain: float32 [768], replicated
- grad_w_router: float32 [768, 8], replicated
- grad_w_in: float32 [8, 768, 3072], P('dp', None, 'tensor')
- grad_w_out: float32 [8, 3072, 768], P('dp', 'tensor')
Inputs may be any that keep to these rules, and one draw needn't show every extreme that they name: `seq_lengths`: entries 2 d and 2 d + 1 are the lengths of the two sequences of index d of dp, placed from its first row in that order; 0 marks an empty second place. The two lengths of a device sum to at most 256, every nonzero length is at least min(48, 256), and some device holds one sequence of exactly 256 tokens. `routes`: routes of unused rows are not read. Among the 256 rows of one device at most 36 name the same expert, a bound that some block reaches.
All inputs are finite; a program needn't handle non-finite values.
Results may differ from a plain program's by a relative error of at most 0.025.
Values may be sent and summed in bfloat16 or wider, within the bound.
A program may use at most 64 MiB of HBM per device.

v0:
```python
import math

import jax
import jax.numpy as jnp
from jax import lax
from jax.sharding import PartitionSpec as P

DH = 64


EPSILON = 1e-06
NEGATIVE = -1e30


def block_size(length):
    return math.gcd(length, 512)


def contract(left, right, left_axis, right_axis):
    return lax.dot_general(
        left, right, (((left_axis,), (right_axis,)), ((), ())), preferred_element_type=jnp.float32
    )


def diagonal_distance(first_row, block_rows, key_count, row_count):
    period = key_count + block_rows
    offsets = jnp.arange(period, dtype=jnp.int32)
    signed = jnp.where(offsets <= key_count - 1, offsets, offsets - period)
    return jnp.clip(first_row - signed, 0, row_count - 1)


def skew_bias(offset_bias, first_row, block_rows, key_count):
    period = key_count + block_rows
    distance = diagonal_distance(first_row, block_rows, key_count, offset_bias.shape[1])
    along = jnp.take(offset_bias, distance, axis=1)
    tiled = jnp.tile(along, (1, block_rows))[:, : block_rows * (period - 1)]
    return tiled.reshape(offset_bias.shape[0], block_rows, period - 1)[:, :, :key_count]


def attention_scores(query_rows, key_rows, offset_bias, segment, first_row, score_scale):
    block_rows = query_rows.shape[0]
    key_count = key_rows.shape[0]
    query_pos = first_row + jnp.arange(block_rows, dtype=jnp.int32)
    key_pos = jnp.arange(key_count, dtype=jnp.int32)
    relative = query_pos[:, None] - key_pos[None, :]
    allowed = (relative >= 0) & (segment[:, None] == segment[None, :])
    bias_grid = skew_bias(offset_bias, first_row, block_rows, key_count)
    scores = (
        jnp.einsum("ihd,jhd->hij", query_rows, key_rows, preferred_element_type=jnp.float32)
        * score_scale
        + bias_grid
    )
    return jnp.where(allowed[None], scores, NEGATIVE)


def bucket_sums(score_grad, first_row, buckets, bucket_count):
    head_count, block_rows, key_count = score_grad.shape
    period = key_count + block_rows
    widened = jnp.pad(score_grad.astype(jnp.float32), ((0, 0), (0, 0), (0, period - 1 - key_count)))
    flat = jnp.pad(
        widened.reshape(head_count, block_rows * (period - 1)), ((0, 0), (0, block_rows))
    )
    diagonal = jnp.sum(flat.reshape(head_count, block_rows, period), axis=1)
    distance = diagonal_distance(first_row, block_rows, key_count, buckets.shape[0])
    pair_bucket = jnp.take(buckets, distance, axis=0)
    pair_onehot = (
        pair_bucket[:, None] == jnp.arange(bucket_count, dtype=jnp.int32)[None, :]
    ).astype(jnp.float32)
    return jnp.transpose(jnp.dot(diagonal, pair_onehot, precision=lax.Precision.HIGHEST))


def on_device(
    activations,
    output_grad,
    seq_lengths,
    routes,
    buckets,
    norm1_gain,
    w_query,
    w_key,
    w_value,
    w_output,
    bias_table,
    norm2_gain,
    w_router,
    w_in,
    w_out,
):
    row_count, quarter = activations.shape
    groups = lax.axis_size("tensor")
    tensor_index = lax.axis_index("tensor")
    experts = lax.axis_size("dp")
    model_width = quarter * groups
    slot_count = max(2, 9 * row_count // (8 * experts))
    head_count = w_query.shape[1] // DH
    score_scale = DH ** (-0.5)
    bucket_count = bias_table.shape[0]

    def to_experts(values):
        return lax.all_to_all(values, "dp", split_axis=0, concat_axis=0, tiled=True)

    def from_experts(values):
        return lax.all_to_all(values, "dp", split_axis=0, concat_axis=0, tiled=True)

    x_full, dy_full, gain_one = (
        lax.all_gather(activations, "tensor", axis=1, tiled=True),
        lax.all_gather(output_grad, "tensor", axis=1, tiled=True),
        lax.all_gather(norm1_gain, "tensor", axis=0, tiled=True),
    )
    position = jnp.arange(row_count, dtype=jnp.int32)
    first_len = seq_lengths[0]
    second_len = seq_lengths[1]
    segment = jnp.where(
        position < first_len, 0, jnp.where(position < first_len + second_len, 1, 2)
    ).astype(jnp.int32)
    live_rows = (segment < 2).astype(jnp.float32)[:, None]
    x_rows = x_full.astype(jnp.float32)
    inv_one = lax.rsqrt(jnp.mean(x_rows * x_rows, axis=1, keepdims=True) + EPSILON)
    gain_full = gain_one.astype(jnp.float32)
    normed_one = (x_rows * inv_one * gain_full).astype(jnp.bfloat16)
    query_rows = (
        jnp.dot(normed_one, w_query, preferred_element_type=jnp.float32)
        .astype(jnp.bfloat16)
        .reshape(row_count, head_count, DH)
    )
    key_rows = (
        jnp.dot(normed_one, w_key, preferred_element_type=jnp.float32)
        .astype(jnp.bfloat16)
        .reshape(row_count, head_count, DH)
    )
    value_rows = (
        jnp.dot(normed_one, w_value, preferred_element_type=jnp.float32)
        .astype(jnp.bfloat16)
        .reshape(row_count, head_count, DH)
    )
    bucket_onehot = buckets[:, None] == jnp.arange(bucket_count, dtype=jnp.int32)[None, :]
    offset_bias = jnp.transpose(
        jnp.dot(bucket_onehot.astype(jnp.bfloat16), bias_table, preferred_element_type=jnp.float32)
    )
    block_rows = block_size(row_count)
    block_index = 0
    begin_row = block_index * block_rows
    scores = attention_scores(query_rows, key_rows, offset_bias, segment, begin_row, score_scale)
    row_max = jnp.max(scores, axis=2, keepdims=True)
    weights = jnp.exp(scores - row_max)
    row_total = jnp.sum(weights, axis=2, keepdims=True)
    weights_low = (weights / row_total).astype(jnp.bfloat16)
    out_blocks = jnp.einsum(
        "hij,jhd->ihd", weights_low, value_rows, preferred_element_type=jnp.float32
    ).astype(jnp.bfloat16)
    lse_blocks = [row_max + jnp.log(row_total)]
    heads_out = out_blocks.reshape(row_count, head_count * DH)
    attn_part = (
        jnp.dot(heads_out, w_output, preferred_element_type=jnp.float32)
        .astype(jnp.bfloat16)
        .astype(jnp.float32)
    )
    attn_rows = lax.psum(attn_part.astype(jnp.bfloat16), "tensor").astype(jnp.float32)
    hidden = x_rows + live_rows * attn_rows
    inv_two = lax.rsqrt(jnp.mean(hidden * hidden, axis=1, keepdims=True) + EPSILON)
    gain_two = norm2_gain.astype(jnp.float32)
    normal_two = hidden * inv_two
    normed_two = (normal_two * gain_two).astype(jnp.bfloat16)
    logits = jnp.dot(normed_two, w_router, preferred_element_type=jnp.float32)
    probs = jax.nn.softmax(logits, axis=1)
    expert_id = routes[:, 0]
    chosen = expert_id[:, None] == jnp.arange(experts, dtype=jnp.int32)[None, :]
    chosen_float = chosen.astype(jnp.float32)
    gate_value = jnp.sum(probs * chosen_float, axis=1, keepdims=True)
    picked = chosen & (segment[:, None] < 2)
    slot_rank = jnp.sum(
        jnp.where(picked, jnp.cumsum(picked.astype(jnp.int32), axis=0) - 1, 0), axis=1
    )
    slot_index = jnp.where(segment < 2, expert_id * slot_count + slot_rank, 0)
    target = jnp.where(segment < 2, expert_id * slot_count + slot_rank, experts * slot_count)
    source_row = (
        jnp.full((experts * slot_count,), row_count, jnp.int32)
        .at[target]
        .set(position, mode="drop")
    )
    filled = source_row < row_count
    source_safe = jnp.minimum(source_row, row_count - 1)

    def pack_slots(values):
        taken_rows = jnp.take(values, source_safe, axis=0)
        return jnp.where(filled[:, None], taken_rows, jnp.zeros_like(taken_rows)).reshape(
            experts, slot_count, values.shape[1]
        )

    dy_rows = dy_full.astype(jnp.float32)
    arrived = to_experts(pack_slots(normed_two))
    expert_rows = arrived.reshape(experts * slot_count, model_width)
    pre_act = jnp.dot(expert_rows, w_in[0], preferred_element_type=jnp.float32)
    activated = jax.nn.gelu(pre_act).astype(jnp.bfloat16)
    expert_part = (
        jnp.dot(activated, w_out[0], preferred_element_type=jnp.float32)
        .astype(jnp.bfloat16)
        .astype(jnp.float32)
    )
    expert_total = lax.psum(expert_part.astype(jnp.bfloat16), "tensor")
    returned = from_experts(expert_total.reshape(experts, slot_count, model_width)).reshape(
        experts * slot_count, model_width
    )
    moe_rows = jnp.take(returned, slot_index, axis=0).astype(jnp.float32) * live_rows
    output_full = hidden + live_rows * gate_value * moe_rows
    output_rows = lax.dynamic_slice_in_dim(output_full, tensor_index * quarter, quarter, 1).astype(
        jnp.bfloat16
    )
    gate_grad = live_rows * jnp.sum(dy_rows * moe_rows, axis=1, keepdims=True)
    moe_grad = (live_rows * gate_value * dy_rows).astype(jnp.bfloat16)
    grad_sent = to_experts(pack_slots(moe_grad)).reshape(experts * slot_count, model_width)
    act_grad = contract(grad_sent, w_out[0], 1, 1)
    gelu_pair = jax.vjp(jax.nn.gelu, pre_act)
    pre_grad = gelu_pair[1](act_grad)[0].astype(jnp.bfloat16)
    w_out_grad = contract(activated, grad_sent, 0, 0)
    w_in_grad = contract(expert_rows, pre_grad, 0, 0)
    rows_grad = contract(pre_grad, w_in[0], 1, 1)
    rows_part = lax.psum_scatter(
        rows_grad.astype(jnp.bfloat16), "tensor", scatter_dimension=1, tiled=True
    )
    came_back = from_experts(rows_part.reshape(experts, slot_count, quarter)).reshape(
        experts * slot_count, quarter
    )
    token_part = jnp.take(came_back, slot_index, axis=0) * live_rows.astype(jnp.bfloat16)
    expert_grad = lax.all_gather(token_part, "tensor", axis=1, tiled=True).astype(jnp.float32)
    logit_grad = (gate_grad * gate_value * (chosen_float - probs)).astype(jnp.bfloat16)
    router_grad = contract(normed_two, logit_grad, 0, 0)
    two_grad = expert_grad + contract(logit_grad, w_router, 1, 1)
    two_gain_grad = jnp.sum(two_grad * normal_two, axis=0)
    scaled_two = two_grad * gain_two
    hidden_grad = dy_rows + inv_two * (
        scaled_two - normal_two * jnp.mean(scaled_two * normal_two, axis=1, keepdims=True)
    )
    attn_grad = (live_rows * hidden_grad).astype(jnp.bfloat16)
    output_w_grad = contract(heads_out, attn_grad, 0, 0)
    heads_grad = (
        contract(attn_grad, w_output, 1, 1).astype(jnp.bfloat16).reshape(row_count, head_count, DH)
    )
    key_total = jnp.zeros((row_count, head_count, DH), jnp.float32)
    value_total = jnp.zeros((row_count, head_count, DH), jnp.float32)
    block_index = 0
    begin_row = block_index * block_rows
    end_row = begin_row + block_rows
    scores = attention_scores(query_rows, key_rows, offset_bias, segment, begin_row, score_scale)
    weights = jnp.exp(scores - lse_blocks[block_index])
    weights_low = weights.astype(jnp.bfloat16)
    weight_grad = jnp.einsum(
        "ihd,jhd->hij", heads_grad, value_rows, preferred_element_type=jnp.float32
    )
    score_grad = (
        weights * (weight_grad - jnp.sum(weights * weight_grad, axis=2, keepdims=True))
    ).astype(jnp.bfloat16)
    query_blocks = (
        jnp.einsum("hij,jhd->ihd", score_grad, key_rows, preferred_element_type=jnp.float32)
        * score_scale
    ).astype(jnp.bfloat16)
    key_total = key_total.at[:end_row].add(
        jnp.einsum("hij,ihd->jhd", score_grad, query_rows, preferred_element_type=jnp.float32)
        * score_scale
    )
    value_total = value_total.at[:end_row].add(
        jnp.einsum("hij,ihd->jhd", weights_low, heads_grad, preferred_element_type=jnp.float32)
    )
    table_grad = bucket_sums(score_grad, begin_row, buckets, bucket_count)
    query_grad = query_blocks.reshape(row_count, head_count * DH)
    key_grad = key_total.astype(jnp.bfloat16).reshape(row_count, head_count * DH)
    value_grad = value_total.astype(jnp.bfloat16).reshape(row_count, head_count * DH)
    query_w_grad = contract(normed_one, query_grad, 0, 0)
    key_w_grad = contract(normed_one, key_grad, 0, 0)
    value_w_grad = contract(normed_one, value_grad, 0, 0)
    one_grad = (
        contract(query_grad, w_query, 1, 1)
        + contract(key_grad, w_key, 1, 1)
        + contract(value_grad, w_value, 1, 1)
    )
    one_part = lax.psum_scatter(
        one_grad.astype(jnp.bfloat16), "tensor", scatter_dimension=1, tiled=True
    ).astype(jnp.float32)
    x_part = activations.astype(jnp.float32)
    gain_part = norm1_gain.astype(jnp.float32)
    normal_part = x_part * inv_one
    scaled_part = one_part * gain_part
    row_mean = (
        lax.psum(jnp.sum(scaled_part * normal_part, axis=1, keepdims=True), "tensor") / model_width
    )
    hidden_part = lax.dynamic_slice_in_dim(hidden_grad, tensor_index * quarter, quarter, 1)
    input_grad = hidden_part + inv_one * (scaled_part - normal_part * row_mean)
    one_gain_grad = jnp.sum(one_part * normal_part, axis=0)
    summed = lax.psum(
        (
            one_gain_grad,
            query_w_grad,
            key_w_grad,
            value_w_grad,
            output_w_grad,
            table_grad,
            two_gain_grad,
            router_grad,
        ),
        "dp",
    )
    return (
        output_rows,
        input_grad,
        summed[0],
        summed[1],
        summed[2],
        summed[3],
        summed[4],
        summed[5],
        summed[6],
        summed[7],
        w_in_grad[None],
        w_out_grad[None],
    )


def solution(mesh):
    in_specs = (
        P("dp", "tensor"),
        P("dp", "tensor"),
        P("dp"),
        P("dp", None),
        P(),
        P("tensor"),
        P(None, "tensor"),
        P(None, "tensor"),
        P(None, "tensor"),
        P("tensor", None),
        P(None, "tensor"),
        P(),
        P(),
        P("dp", None, "tensor"),
        P("dp", "tensor", None),
    )
    out_specs = (
        P("dp", "tensor"),
        P("dp", "tensor"),
        P("tensor"),
        P(None, "tensor"),
        P(None, "tensor"),
        P(None, "tensor"),
        P("tensor", None),
        P(None, "tensor"),
        P(),
        P(),
        P("dp", None, "tensor"),
        P("dp", "tensor", None),
    )
    return jax.shard_map(
        on_device, mesh=mesh, in_specs=in_specs, out_specs=out_specs, check_vma=False
    )
```

profile of v0, /device:TPU:14, one launch (start us, length us, event | category | flops | bytes accessed | tf_op | source)
XLA Modules:
  0.0 390.9 jit_solution(13494488372413971125)
XLA Ops:
  7.3 6.5 %all_gather.12 = bf16[256,768]{0,1:T(8,128)(2,1)S(1)} all-gather(bf16[256,192]{0,1:T(8,128)(2,1)} %param.27), channel_id=1, replica_groups=mesh['dp'=8,'tensor'=4] {'tensor'}, dimensions={1}, use_global_device_ids=true | all-gather | bytes 491520 | tf_op jit(solution)/shard_map/all_gather | solution.py:106
  15.5 6.4 %all-reduce.2 = bf16[768]{0:T(1024)(128)(2,1)S(1)} all-reduce(bf16[768]{0:T(1024)(128)(2,1)S(1)} %dynamic-update-slice.4), channel_id=1, replica_groups=mesh['dp'=8,'tensor'=4] {'tensor'}, use_global_device_ids=true, to_apply=%add.2 | all-reduce | flops 768 | bytes 3072
  25.1 1.7 slice.76
  26.8 4.5 %reshape.385 = f32[3,256,511]{2,1,0:T(8,128)} reshape(f32[3,130816]{1,0:T(4,128)} %slice.76) | data formatting | bytes 3139584 | tf_op jit(solution)/shard_map/reshape | solution.py:37
  32.7 2.0 convolution_convert_fusion.8
  41.0 1.2 convert_convert_fusion
  44.6 1.4 scatter_custom_fusion
  46.0 27.9 %all-reduce.9.cloned.1.call-done = bf16[256,768]{1,0:T(8,128)(2,1)} async-done(((bf16[256,768]{1,0:T(8,128)(2,1)}), bf16[256,768]{1,0:T(8,128)(2,1)}) %all-reduce.9.cloned.1.call-update) | async-done | bytes 393232 | tf_op jit(solution)/shard_map/psum | solution.py:158
  73.9 1.3 multiply_reduce_fusion.3
  76.3 2.1 gather_fusion.4
  79.3 1.9 reshape.388
  81.2 6.0 %all-to-all-start = ((bf16[8,36,768]{2,1,0:T(8,128)(2,1)}), bf16[8,36,768]{2,1,0:T(8,128)(2,1)}, u32[]{:S(2)}, u32[]{:S(2)}) async-start(bf16[8,36,768]{2,1,0:T(8,128)(2,1)} %reshape.388), calls=%async_computation | async-start | bytes 983040 | tf_op jit(solution)/shard_map/all_to_all | solution.py:100
  87.2 6.5 %all_gather.14 = bf16[256,768]{0,1:T(8,128)(2,1)S(1)} all-gather(bf16[256,192]{0,1:T(8,128)(2,1)S(1)} %copy-done.34), channel_id=1, replica_groups=mesh['dp'=8,'tensor'=4] {'tensor'}, dimensions={1}, use_global_device_ids=true | all-gather | bytes 491520 | tf_op jit(solution)/shard_map/all_gather | solution.py:107
  94.7 3.2 all-to-all-done
  99.0 1.9 fusion.8
  101.9 1.4 convolution_convert_fusion.1
  103.3 1.9 reshape.390
  105.9 32.8 %all-reduce.11.cloned.1.call-done = bf16[8,36,768]{2,1,0:T(8,128)(2,1)} async-done(((bf16[8,36,768]{2,1,0:T(8,128)(2,1)}), bf16[8,36,768]{2,1,0:T(8,128)(2,1)}) %all-reduce.11.cloned.1.call-update) | async-done | bytes 442384 | tf_op jit(solution)/shard_map/psum | solution.py:200
  138.7 6.2 %all-to-all-start.1 = ((bf16[8,36,768]{2,1,0:T(8,128)(2,1)}), bf16[8,36,768]{2,1,0:T(8,128)(2,1)}, u32[]{:S(2)}, u32[]{:S(2)}) async-start(bf16[8,36,768]{2,1,0:T(8,128)(2,1)} %all-reduce.11.cloned.1.call-done), calls=%async_computation.1 | async-start | bytes 983040 | tf_op jit(solution)/shard_map/all_to_all | solution.py:103
  145.3 9.7 %all-to-all-done.1 = bf16[8,36,768]{2,1,0:T(8,128)(2,1)} async-done(((bf16[8,36,768]{2,1,0:T(8,128)(2,1)}), bf16[8,36,768]{2,1,0:T(8,128)(2,1)}, u32[]{:S(2)}, u32[]{:S(2)}) %all-to-all-start.1) | async-done | bytes 442400 | tf_op jit(solution)/shard_map/all_to_all | solution.py:103
  156.1 1.9 gather_fusion
  158.1 2.9 fusion.25
  161.0 2.6 gather_fusion.5
  165.6 6.5 %all-to-all-start.2 = ((bf16[8,36,768]{2,1,0:T(8,128)(2,1)}), bf16[8,36,768]{2,1,0:T(8,128)(2,1)S(1)}, u32[]{:S(2)}, u32[]{:S(2)}) async-start(bf16[8,36,768]{2,1,0:T(8,128)(2,1)} %reshape.392), calls=%async_computation.2 | async-start | bytes 983040 | tf_op jit(solution)/shard_map/all_to_all | solution.py:100
  173.4 4.7 %gather_fusion.2 = s32[512]{0:T(512)} fusion(s32[256]{0:T(256)S(1)} %copy-done.1, s32[1024]{0:T(1024)S(1)} %pad_clamp_fusion), kind=kCustom, calls=%fused_computation.5 | custom fusion | bytes 6144 | tf_op jit(solution)/shard_map/jit(_take)/gather | solution.py:65
  178.1 4.3 %all-to-all-done.2 = bf16[8,36,768]{2,1,0:T(8,128)(2,1)S(1)} async-done(((bf16[8,36,768]{2,1,0:T(8,128)(2,1)}), bf16[8,36,768]{2,1,0:T(8,128)(2,1)S(1)}, u32[]{:S(2)}, u32[]{:S(2)}) %all-to-all-start.2) | async-done | bytes 442400 | tf_op jit(solution)/shard_map/all_to_all | solution.py:100
  183.2 2.2 fusion.18
  186.3 1.3 convolution_convert_fusion
  187.6 2.1 copy.93
  189.7 1.3 broadcast_select_fusion
  191.0 1.9 fusion.36
  192.9 1.6 copy.87
  195.8 1.5 fusion.54
  197.3 15.1 %reduce-scatter.7.cloned.1.call-done = bf16[192,288]{1,0:T(8,128)(2,1)} async-done(((bf16[768,288]{1,0:T(8,128)(2,1)}), bf16[192,288]{1,0:T(8,128)(2,1)}) %reduce-scatter.7.cloned.1.call-update) | async-done | bytes 110608
  214.1 6.0 %all-to-all-start.3 = ((bf16[8,36,192]{2,1,0:T(8,128)(2,1)}), bf16[8,36,192]{2,1,0:T(8,128)(2,1)S(1)}, u32[]{:S(2)}, u32[]{:S(2)}) async-start(bf16[8,36,192]{2,1,0:T(8,128)(2,1)} %reshape.394), calls=%async_computation.3 | async-start | bytes 327680 | tf_op jit(solution)/shard_map/all_to_all | solution.py:103
  220.2 3.7 convolution_bitcast_fusion
  223.8 2.2 convolution_bitcast_fusion.1
  226.1 1.3 gather_fusion.1
  227.5 6.9 %all_gather.15 = bf16[256,768]{0,1:T(8,128)(2,1)} all-gather(bf16[256,192]{0,1:T(8,128)(2,1)S(1)} %select_multiply_fusion), channel_id=1, replica_groups=mesh['dp'=8,'tensor'=4] {'tensor'}, dimensions={1}, use_global_device_ids=true | all-gather | bytes 491520 | tf_op jit(solution)/shard_map/all_gather | solution.py:225
  234.4 1.2 copy.80
  235.6 1.9 multiply_reduce_fusion
  245.7 1.6 reshape.398
  247.4 2.1 fusion.58
  253.2 11.8 %reduce-scatter.9.cloned.1.call-done = bf16[192,256]{1,0:T(8,128)(2,1)} async-done(((bf16[768,256]{1,0:T(8,128)(2,1)}), bf16[192,256]{1,0:T(8,128)(2,1)}) %reduce-scatter.9.cloned.1.call-update) | async-done | bytes 98320
  266.3 6.8 %psum.79 = f32[256,1]{0,1:T(1,128)S(1)} all-reduce(f32[256,1]{0,1:T(1,128)S(1)} %bitcast.132), channel_id=1, replica_groups=mesh['dp'=8,'tensor'=4] {'tensor'}, use_global_device_ids=true, to_apply=%region_19.22 | all-reduce | flops 256 | bytes 2048 | tf_op jit(solution)/shard_map/psum | solution.py:284
  274.1 31.9 %all-reduce.3 = (f32[192]{0:T(256)}, f32[32,3]{0,1:T(4,128)}, f32[768]{0:T(1024)}, f32[768,8]{0,1:T(8,128)}) all-reduce(f32[192]{0:T(256)S(1)} %get-tuple-element.104, f32[32,3]{0,1:T(4,128)S(1)} %fusion.38, f32[768]{0:T(1024)S(1)} %copy-done.44, f32[768,8]{0,1:T(8,128)S(1)} %copy-done.35), channel_id=1, replica_groups=mesh['dp'=8,'tensor'=4] {'dp'}, use_global_device_ids=true, to_apply=%region_21.24 | all-reduce | flops 7200 | bytes 57600 | tf_op jit(solution)/shard_map/psum | solution.py:289
  306.0 73.9 %all-reduce.13.cloned.1.call-done = (f32[768,192]{0,1:T(8,128)}, f32[768,192]{0,1:T(8,128)}, f32[768,192]{0,1:T(8,128)}, f32[192,768]{1,0:T(8,128)}) async-done(((f32[768,192]{0,1:T(8,128)}, f32[768,192]{0,1:T(8,128)}, f32[768,192]{0,1:T(8,128)}, f32[192,768]{1,0:T(8,128)}), (f32[768,192]{0,1:T(8,128)}, f32[768,192]{0,1:T(8,128)}, f32[768,192]{0,1:T(8,128)}, ...) | async-done | bytes 2359312 | tf_op jit(solution)/shard_map/psum | solution.py:289
  379.9 2.0 copy.109
  (237 shorter events, 44.5 us)
Async XLA Ops:
  7.2 94.7 %copy-start = (bf16[1,768,768]{2,1,0:T(8,128)(2,1)S(1)}, bf16[1,768,768]{2,1,0:T(8,128)(2,1)}, u32[]{:S(2)}) copy-start(bf16[1,768,768]{2,1,0:T(8,128)(2,1)} %param.41) | copy-start | bytes 3538948
  7.2 6.8 %copy-start.64 = (u32[32]{0:T(128)S(1)}, u32[32]{0:T(128)}, u32[]{:S(2)}) copy-start(u32[32]{0:T(128)} %constant.215) | copy-start | bytes 388
  7.2 8.1 %copy-start.62 = (bf16[192]{0:T(256)(128)(2,1)S(1)}, bf16[192]{0:T(256)(128)(2,1)}, u32[]{:S(2)}) copy-start(bf16[192]{0:T(256)(128)(2,1)} %param.32) | copy-start | bytes 1156
  7.2 14.9 %copy-start.61 = (bf16[32,3]{0,1:T(4,128)(2,1)S(1)}, bf16[32,3]{0,1:T(4,128)(2,1)}, u32[]{:S(2)}) copy-start(bf16[32,3]{0,1:T(4,128)(2,1)} %param.37) | copy-start | bytes 580
  7.2 14.9 %copy-start.1 = (s32[256]{0:T(256)S(1)}, s32[256]{0:T(256)}, u32[]{:S(2)}) copy-start(s32[256]{0:T(256)} %param.31) | copy-start | bytes 3076
  7.2 66.7 %all-reduce.9.cloned.1.call-start = ((), (), s32[]{:S(2)}) async-start(), calls=%async_computation.6 | async-start | bytes 786432 | tf_op jit(solution)/shard_map/psum | solution.py:158
  22.1 12.9 %copy-start.40 = (f32[256]{0:T(256)}, f32[256]{0:T(256)S(1)}, u32[]{:S(2)}) copy-start(f32[256]{0:T(256)S(1)} %add_rsqrt_fusion.1) | copy-start | bytes 3076
  32.4 2.3 copy-start.27
  32.6 2.4 copy-start.29
  35.1 3.4 copy-start.20
  35.5 3.2 copy-start.22
  39.3 3.6 copy-start.58
  39.3 3.6 copy-start.38
  42.2 103.1 %copy-start.53 = (pred[256]{0:T(512)(128)(4,1)}, pred[256]{0:T(512)(128)(4,1)S(1)}, u32[]{:S(2)}) copy-start(pred[256]{0:T(512)(128)(4,1)S(1)} %get-tuple-element.115) | copy-start | bytes 772
  42.9 115.2 %copy-start.45 = (f32[256]{0:T(256)}, f32[256]{0:T(256)S(1)}, u32[]{:S(2)}) copy-start(f32[256]{0:T(256)S(1)} %convert_element_type.159) | copy-start | bytes 3076
  42.9 32.4 %copy-start.36 = (f32[768]{0:T(1024)}, f32[768]{0:T(1024)S(1)}, u32[]{:S(2)}) copy-start(f32[768]{0:T(1024)S(1)} %convert_element_type.170) | copy-start | bytes 9220
  75.3 3.1 copy-start.47
  79.3 8.0 %copy-start.34 = (bf16[256,192]{0,1:T(8,128)(2,1)S(1)}, bf16[256,192]{0,1:T(8,128)(2,1)}, u32[]{:S(2)}) copy-start(bf16[256,192]{0,1:T(8,128)(2,1)} %param.28) | copy-start | bytes 294916
  81.2 16.7 %all-to-all-start = ((bf16[8,36,768]{2,1,0:T(8,128)(2,1)}), bf16[8,36,768]{2,1,0:T(8,128)(2,1)}, u32[]{:S(2)}, u32[]{:S(2)}) async-start(bf16[8,36,768]{2,1,0:T(8,128)(2,1)} %reshape.388), calls=%async_computation | async-start | bytes 983040 | tf_op jit(solution)/shard_map/all_to_all | solution.py:100
  87.2 51.5 %all-reduce.11.cloned.1.call-start = ((), (), s32[]{:S(2)}) async-start(), calls=%async_computation.7 | async-start | bytes 983040 | tf_op jit(solution)/shard_map/psum | solution.py:200
  99.0 2.0 copy-start.6
  103.3 41.6 %copy-start.39 = (bf16[768,8]{0,1:T(8,128)(2,1)S(1)}, bf16[768,8]{0,1:T(8,128)(2,1)}, u32[]{:S(2)}) copy-start(bf16[768,8]{0,1:T(8,128)(2,1)} %param.39) | copy-start | bytes 36868
  105.9 52.2 %copy-start.54 = (pred[256]{0:T(512)(128)(4,1)}, pred[256]{0:T(512)(128)(4,1)S(1)}, u32[]{:S(2)}) copy-start(pred[256]{0:T(512)(128)(4,1)S(1)} %get-tuple-element.116) | copy-start | bytes 772
  138.7 16.3 %all-to-all-start.1 = ((bf16[8,36,768]{2,1,0:T(8,128)(2,1)}), bf16[8,36,768]{2,1,0:T(8,128)(2,1)}, u32[]{:S(2)}, u32[]{:S(2)}) async-start(bf16[8,36,768]{2,1,0:T(8,128)(2,1)} %all-reduce.11.cloned.1.call-done), calls=%async_computation.1 | async-start | bytes 983040 | tf_op jit(solution)/shard_map/all_to_all | solution.py:103
  144.9 13.2 %copy-start.52 = (s32[1024]{0:T(1024)}, s32[1024]{0:T(1024)S(1)}, u32[]{:S(2)}) copy-start(s32[1024]{0:T(1024)S(1)} %pad_clamp_fusion.1) | copy-start | bytes 12292
  145.2 12.9 %copy-start.42 = (f32[256]{0:T(256)}, f32[256]{0:T(256)S(1)}, u32[]{:S(2)}) copy-start(f32[256]{0:T(256)S(1)} %get-tuple-element.129) | copy-start | bytes 3076
  145.2 12.8 %copy-start.43 = (f32[256]{0:T(256)}, f32[256]{0:T(256)S(1)}, u32[]{:S(2)}) copy-start(f32[256]{0:T(256)S(1)} %fusion.46) | copy-start | bytes 3076
  145.3 12.8 %copy-start.51 = (f32[256]{0:T(256)}, f32[256]{0:T(256)S(1)}, u32[]{:S(2)}) copy-start(f32[256]{0:T(256)S(1)} %select_reduce_fusion) | copy-start | bytes 3076
  145.3 12.8 %copy-start.50 = (f32[256]{0:T(256)}, f32[256]{0:T(256)S(1)}, u32[]{:S(2)}) copy-start(f32[256]{0:T(256)S(1)} %broadcast_select_fusion.1) | copy-start | bytes 3076
  164.7 7.3 %copy-start.26 = (bf16[256,192]{0,1:T(8,128)(2,1)S(1)}, bf16[256,192]{0,1:T(8,128)(2,1)}, u32[]{:S(2)}) copy-start(bf16[256,192]{0,1:T(8,128)(2,1)} %param.27) | copy-start | bytes 294916
  164.7 8.1 %copy-start.63 = (bf16[192]{0:T(256)(128)(2,1)S(1)}, bf16[192]{0:T(256)(128)(2,1)}, u32[]{:S(2)}) copy-start(bf16[192]{0:T(256)(128)(2,1)} %param.32) | copy-start | bytes 1156
  165.6 16.8 %all-to-all-start.2 = ((bf16[8,36,768]{2,1,0:T(8,128)(2,1)}), bf16[8,36,768]{2,1,0:T(8,128)(2,1)S(1)}, u32[]{:S(2)}, u32[]{:S(2)}) async-start(bf16[8,36,768]{2,1,0:T(8,128)(2,1)} %reshape.392), calls=%async_computation.2 | async-start | bytes 983040 | tf_op jit(solution)/shard_map/all_to_all | solution.py:100
  172.1 40.3 %reduce-scatter.7.cloned.1.call-start = ((), (), s32[]{:S(2)}) async-start(), calls=%async_computation.8 | async-start | bytes 737280
  183.2 3.0 copy-start.10
  187.6 3.4 copy-start.3
  214.1 11.9 %all-to-all-start.3 = ((bf16[8,36,192]{2,1,0:T(8,128)(2,1)}), bf16[8,36,192]{2,1,0:T(8,128)(2,1)S(1)}, u32[]{:S(2)}, u32[]{:S(2)}) async-start(bf16[8,36,192]{2,1,0:T(8,128)(2,1)} %reshape.394), calls=%async_computation.3 | async-start | bytes 327680 | tf_op jit(solution)/shard_map/all_to_all | solution.py:103
  220.2 44.9 %reduce-scatter.9.cloned.1.call-start = ((), (), s32[]{:S(2)}) async-start(), calls=%async_computation.9 | async-start | bytes 491520
  220.2 3.7 copy-start.7
  220.2 3.7 copy-start.19
  244.1 135.8 %all-reduce.13.cloned.1.call-start = ((), (), s32[]{:S(2)}) async-start(), calls=%async_computation.10 | async-start | bytes 4718592 | tf_op jit(solution)/shard_map/psum | solution.py:289
  247.4 3.3 copy-start.5
  247.4 3.3 copy-start.25
  252.3 13.7 %copy-start.13 = (bf16[256,192]{1,0:T(8,128)(2,1)S(1)}, bf16[256,192]{1,0:T(8,128)(2,1)}, u32[]{:S(2)}) copy-start(bf16[256,192]{1,0:T(8,128)(2,1)} %copy.85) | copy-start | bytes 294916
  252.3 13.7 %copy-start.56 = (f32[192]{0:T(256)S(1)}, f32[192]{0:T(256)}, u32[]{:S(2)}) copy-start(f32[192]{0:T(256)} %convert_element_type.199) | copy-start | bytes 2308
  253.0 21.2 %copy-start.35 = (f32[768,8]{0,1:T(8,128)S(1)}, f32[768,8]{0,1:T(8,128)}, u32[]{:S(2)}) copy-start(f32[768,8]{0,1:T(8,128)} %fusion.54) | copy-start | bytes 73732
  253.0 21.2 %copy-start.44 = (f32[768]{0:T(1024)S(1)}, f32[768]{0:T(1024)}, u32[]{:S(2)}) copy-start(f32[768]{0:T(1024)} %get-tuple-element.102) | copy-start | bytes 9220
  379.9 2.0 copy-start.17
  379.9 2.8 copy-start.16
  (27 other events, 30.9 us)
Sparse Core Ops, SparseCore 0:
  41.2 32.6 all-reduce.8
  105.3 33.3 all-reduce.10
  189.9 22.4 reduce-scatter.6
  244.2 20.7 reduce-scatter.8
  269.4 110.4 all-reduce.12
where the time goes:
time: 395 us; the launch traced here: 391 us
  waiting for transfers between devices  179 us (45%)
  blocking collectives  65 us (16%)
  local copies, waits for them, and re-layouts  57.6 us (15%)
  matrix products  30 us (8%)
  starting transfers between devices  25 us (6%)
  other arithmetic  17.7 us (4%)
  between operations  16.7 us (4%)
    psum x1, waiting for transfers between devices, on_device(): lax.psum((one_gain_grad, query_w_grad, key_w_grad, value_w_grad, output_w...  73.9 us
    psum x1, waiting for transfers between devices, on_device(): expert_total = lax.psum(expert_part.astype(jnp.bfloat16), 'tensor')  32.8 us
    psum x1, blocking collectives, on_device(): lax.psum((one_gain_grad, query_w_grad, key_w_grad, value_w_grad, output_w...  31.9 us
    psum x1, waiting for transfers between devices, on_device(): lax.psum(attn_part.astype(jnp.bfloat16), 'tensor').astype(jnp.float32)  27.9 us
    unnamed x7, waiting for transfers between devices  27 us
    unnamed x147, local copies, waits for them, and re-layouts  21.8 us
    dot_general x14, matrix products, contract(): lax.dot_general(left, right, (((left_axis,), (right_axis,)), ((), ())), p...  20.4 us
    all_to_all x2, starting transfers between devices, to_experts(): return lax.all_to_all(values, 'dp', split_axis=0, concat_axis=0, tiled=True)  12.5 us
  transfers between devices with their start and end apart: 9, of which 8 were waited for; matrix products, arithmetic and copies ran while one was open for 9% of the time, Pallas kernels for 0%

commit v1 on v0

v1 whole, which is shorter than its diff:
```python
import functools
import math

import jax
import jax.numpy as jnp
from jax import lax
from jax.experimental import pallas as pl
from jax.experimental.pallas import tpu as pltpu
from jax.sharding import PartitionSpec as P

DH = 64
EPSILON = 1e-06
NEGATIVE = -1e30
F32 = jnp.float32
BF16 = jnp.bfloat16
MESH = pl.DeviceIdType.MESH


def dot(left, right, left_axis=1, right_axis=0):
    return lax.dot_general(
        left, right, (((left_axis,), (right_axis,)), ((), ())), preferred_element_type=F32
    )


def iota(shape, axis):
    return lax.broadcasted_iota(jnp.int32, shape, axis)


def kernel(
    n_dp, n_t, slots, pad,
    lens_ref, x_ref, dy_ref, routes_ref, buckets_ref, gain1_ref, wq_ref, wk_ref, wv_ref, wo_ref,
    table_ref, gain2_ref, wr_ref, win_ref, wout_ref,
    out_ref, dx_ref, dgain1_ref, dwq_ref, dwk_ref, dwv_ref, dwo_ref, dtable_ref, dgain2_ref,
    dwr_ref, dwin_ref, dwout_ref,
    xs, gs, a_send, a_recv, a_sum, sent, arrived, parts, parts_in, back, back_in,
    eg_all, row_part, row_in, one_send, one_in, row2_part, row2_in,
    grads, grads_in, grads_all, small1, small2, small1_in, small2_in,
    quarters, p_ref, activated, pre_grad,
    t_send, t_recv, d_send, d_recv, local_sem,
):
    me_d = lax.axis_index("dp")
    me_t = lax.axis_index("tensor")
    rows, quarter = x_ref.shape
    width = quarter * n_t
    head_count = wq_ref.shape[1] // DH
    scale = DH ** (-0.5)
    bucket_count = table_ref.shape[0]
    total_slots = n_dp * pad

    barrier = pltpu.get_barrier_semaphore()
    for k in range(1, n_t):
        pl.semaphore_signal(
            barrier, inc=1, device_id=(me_d, lax.rem(me_t + k, n_t)), device_id_type=MESH
        )

    def greet(k, carry):
        pl.semaphore_signal(
            barrier, inc=1, device_id=(lax.rem(me_d + k, n_dp), me_t), device_id_type=MESH
        )
        return carry

    lax.fori_loop(1, n_dp, greet, 0)
    pl.semaphore_wait(barrier, n_t - 1 + n_dp - 1)

    def over_tensor(phase, source, target):
        copies = []
        for k in range(1, n_t):
            peer = lax.rem(me_t + k, n_t)
            copy = pltpu.make_async_remote_copy(
                src_ref=source(peer),
                dst_ref=target,
                send_sem=t_send.at[phase, k],
                recv_sem=t_recv.at[phase, k],
                device_id=(me_d, peer),
                device_id_type=MESH,
            )
            copy.start()
            copies.append(copy)
        return copies

    def finish(copies):
        for copy in copies:
            copy.wait()

    def dp_copy(phase, k, source, target, peer):
        return pltpu.make_async_remote_copy(
            src_ref=source(peer),
            dst_ref=target,
            send_sem=d_send.at[phase, k],
            recv_sem=d_recv.at[phase, k],
            device_id=(peer, me_t),
            device_id_type=MESH,
        )

    def dp_start(phase, source, target):
        def body(k, carry):
            dp_copy(phase, k, source, target, lax.rem(me_d + k, n_dp)).start()
            return carry

        lax.fori_loop(1, n_dp, body, 0)

    def dp_wait(phase, source, target):
        def body(k, carry):
            dp_copy(phase, k, source, target, lax.rem(me_d + k, n_dp)).wait()
            return carry

        lax.fori_loop(1, n_dp, body, 0)

    xs[me_t, 0] = x_ref[...]
    xs[me_t, 1] = dy_ref[...]
    gs[me_t] = jnp.broadcast_to(gain1_ref[...].astype(F32), (16, quarter)).astype(BF16)
    first = over_tensor(0, lambda p: xs.at[me_t], xs.at[me_t])
    first += over_tensor(1, lambda p: gs.at[me_t], gs.at[me_t])

    first_len = lens_ref[0]
    both_len = first_len + lens_ref[1]
    row_col = iota((rows, 1), 0)
    row_row = iota((1, rows), 1)

    def segment_of(position):
        return jnp.where(position < first_len, 0, jnp.where(position < both_len, 1, 2))

    live = (row_col < both_len).astype(F32)
    at_i = iota((rows, rows), 0)
    at_j = iota((rows, rows), 1)
    allowed = (at_i >= at_j) & (segment_of(row_col) == segment_of(row_row))
    eye = at_i == at_j
    flip = (lax.rem(at_i + at_j, rows) == 0).astype(F32).astype(BF16)
    chosen = (routes_ref[...] == iota((rows, n_dp), 1)).astype(F32)
    picked = chosen * live
    earlier = dot((at_j < at_i).astype(F32).astype(BF16), picked.astype(BF16))
    rank = jnp.sum(picked * earlier, axis=1, keepdims=True)
    slot = routes_ref[...].astype(F32) * pad + rank
    slot = jnp.where(live > 0, slot, -1.0)
    unpack = (slot == iota((rows, total_slots), 1).astype(F32)).astype(F32).astype(BF16)
    bucket_hot = (iota((bucket_count, rows), 0) == buckets_ref[...]).astype(F32)
    offset_bias = dot(table_ref[...], dot(bucket_hot.astype(BF16), flip).astype(BF16), 0, 0)

    finish(first)
    x_full = jnp.concatenate([xs[q, 0].astype(F32) for q in range(n_t)], axis=1)
    dy_full = jnp.concatenate([xs[q, 1].astype(F32) for q in range(n_t)], axis=1)
    gain1 = jnp.concatenate([gs[q].astype(F32)[0:1] for q in range(n_t)], axis=1)
    inv_one = lax.rsqrt(jnp.mean(x_full * x_full, axis=1, keepdims=True) + EPSILON)
    normed_one = (x_full * inv_one * gain1).astype(BF16)
    query = dot(normed_one, wq_ref[...]).astype(BF16)
    key = dot(normed_one, wk_ref[...]).astype(BF16)
    value = dot(normed_one, wv_ref[...]).astype(BF16)

    def head(values, h):
        return values[:, h * DH : (h + 1) * DH]

    outs = []
    attn_part = jnp.zeros((rows, width), F32)
    for h in range(head_count):
        bias = jnp.broadcast_to(offset_bias[h : h + 1], (rows, rows))
        bias = pltpu.roll(bias, 0, 1, stride=1, stride_axis=0)
        scores = dot(head(query, h), head(key, h), 1, 1) * scale + bias
        scores = jnp.where(allowed, scores, NEGATIVE)
        weights = jnp.exp(scores - jnp.max(scores, axis=1, keepdims=True))
        weights = weights / jnp.sum(weights, axis=1, keepdims=True)
        p_ref[h] = weights
        outs.append(dot(weights.astype(BF16), head(value, h)).astype(BF16))
        attn_part += dot(outs[h], wo_ref[h * DH : (h + 1) * DH])

    share = rows // n_t
    a_send[...] = attn_part.astype(BF16).reshape(n_t, share, width)
    a_recv[me_t] = a_send[me_t]
    finish(over_tensor(2, lambda p: a_send.at[p], a_recv.at[me_t]))
    a_total = a_recv[0].astype(F32)
    for q in range(1, n_t):
        a_total += a_recv[q].astype(F32)
    a_sum[me_t] = a_total.astype(BF16)
    finish(over_tensor(3, lambda p: a_sum.at[me_t], a_sum.at[me_t]))
    hidden = x_full + live * a_sum[...].reshape(rows, width).astype(F32)
    inv_two = lax.rsqrt(jnp.mean(hidden * hidden, axis=1, keepdims=True) + EPSILON)
    gain2 = gain2_ref[...].astype(F32)
    normal_two = hidden * inv_two
    normed_two = (normal_two * gain2).astype(BF16)
    logits = dot(normed_two, wr_ref[...])
    probs = jnp.exp(logits - jnp.max(logits, axis=1, keepdims=True))
    probs = probs / jnp.sum(probs, axis=1, keepdims=True)
    gate = jnp.sum(probs * chosen, axis=1, keepdims=True)
    moe_grad = (live * gate * dy_full).astype(BF16)

    sent[:, 0] = dot(unpack, normed_two, 0, 0).astype(BF16).reshape(n_dp, pad, width)
    sent[:, 1] = dot(unpack, moe_grad, 0, 0).astype(BF16).reshape(n_dp, pad, width)
    arrived[me_d] = sent[me_d]
    dispatch = (0, lambda p: sent.at[p], arrived.at[me_d])
    dp_start(*dispatch)
    for q in range(n_t):
        quarters[q] = hidden[:, q * quarter : (q + 1) * quarter]
    dp_wait(*dispatch)
    root = math.sqrt(2.0 / math.pi)
    step = total_slots if total_slots <= 512 else 256
    for begin in range(0, total_slots, step):
        span = slice(begin, begin + step)
        sources = slice(begin // pad, (begin + step) // pad)
        pre = dot(arrived[sources, 0].reshape(step, width), win_ref[0])
        square = pre * pre
        bent = jnp.tanh(root * (pre + 0.044715 * square * pre))
        activated[span] = (0.5 * pre * (1.0 + bent)).astype(BF16)
        slope = 0.5 * (1.0 + bent) + 0.5 * pre * (1.0 - bent * bent) * root * (
            1.0 + 3 * 0.044715 * square
        )
        wide = dot(activated[span], wout_ref[0])
        for q in range(n_t):
            parts[q, 0, span] = wide[:, q * quarter : (q + 1) * quarter].astype(BF16)
        act_grad = dot(arrived[sources, 1].reshape(step, width), wout_ref[0], 1, 1)
        pre_grad[span] = (act_grad * slope).astype(BF16)
        wide = dot(pre_grad[span], win_ref[0], 1, 1)
        for q in range(n_t):
            parts[q, 1, span] = wide[:, q * quarter : (q + 1) * quarter].astype(BF16)
    parts_in[me_t] = parts[me_t]
    shares = over_tensor(4, lambda p: parts.at[p], parts_in.at[me_t])
    dwout_ref[0] = dot(activated[...], arrived[:, 1].reshape(total_slots, width), 0, 0)
    dwin_ref[0] = dot(arrived[:, 0].reshape(total_slots, width), pre_grad[...], 0, 0)
    finish(shares)
    for s in range(2):
        total = parts_in[0, s].astype(F32)
        for q in range(1, n_t):
            total += parts_in[q, s].astype(F32)
        back[:, s] = total.astype(BF16).reshape(n_dp, pad, quarter)

    back_in[me_d] = back[me_d]
    home = (1, lambda p: back.at[p], back_in.at[me_d])
    dp_start(*home)
    dp_wait(*home)
    moe_quarter = dot(unpack, back_in[:, 0].reshape(total_slots, quarter))
    eg_all[me_t] = dot(unpack, back_in[:, 1].reshape(total_slots, quarter)).astype(BF16)

    def to_row(column):
        return jnp.sum(jnp.where(eye, column, 0.0), axis=0, keepdims=True)

    def to_column(line):
        return jnp.sum(jnp.where(eye, line, 0.0), axis=1, keepdims=True)

    gate_part = jnp.sum(xs[me_t, 1].astype(F32) * moe_quarter, axis=1, keepdims=True)
    row_part[...] = jnp.broadcast_to(to_row(gate_part), (8, rows))
    row_in[me_t] = row_part[...]
    sixth = over_tensor(5, lambda p: eg_all.at[me_t], eg_all.at[me_t])
    sixth += over_tensor(6, lambda p: row_part, row_in.at[me_t])
    out_ref[...] = (quarters[me_t] + live * gate * moe_quarter).astype(BF16)
    finish(sixth)
    row_total = row_in[0]
    for q in range(1, n_t):
        row_total += row_in[q]
    gate_grad = live * to_column(row_total[0:1])
    expert_grad = jnp.concatenate([eg_all[q].astype(F32) for q in range(n_t)], axis=1)
    logit_grad = (gate_grad * gate * (chosen - probs)).astype(BF16)
    two_grad = expert_grad + dot(logit_grad, wr_ref[...], 1, 1)
    small1[0:8] = jnp.broadcast_to(
        jnp.sum(two_grad * normal_two, axis=0, keepdims=True), (8, width)
    ).astype(BF16)
    small1[8 : 8 + n_dp] = dot(logit_grad, normed_two, 0, 0).astype(BF16)
    if 8 + n_dp < small1.shape[0]:
        small1[8 + n_dp :] = jnp.zeros((small1.shape[0] - 8 - n_dp, width), BF16)
    small1_in[me_d] = small1[...]
    small_one = (2, lambda p: small1, small1_in.at[me_d])
    dp_start(*small_one)
    scaled_two = two_grad * gain2
    hidden_grad = dy_full + inv_two * (
        scaled_two - normal_two * jnp.mean(scaled_two * normal_two, axis=1, keepdims=True)
    )
    attn_grad = (live * hidden_grad).astype(BF16)
    for q in range(n_t):
        quarters[q] = hidden_grad[:, q * quarter : (q + 1) * quarter]
    heads_grad = dot(attn_grad, wo_ref[...], 1, 1).astype(BF16)

    own = head_count * DH
    one_grad = jnp.zeros((rows, width), F32)
    small2[...] = jnp.zeros(small2.shape, F32)
    for h in range(head_count):
        lo = h * DH
        grads[3 * own + lo : 3 * own + lo + DH] = dot(outs[h], attn_grad, 0, 0).astype(BF16)
        weights = p_ref[h]
        grad_h = head(heads_grad, h)
        weight_grad = dot(grad_h, head(value, h), 1, 1)
        score_grad = (
            weights * (weight_grad - jnp.sum(weights * weight_grad, axis=1, keepdims=True))
        ).astype(BF16)
        query_grad = (dot(score_grad, head(key, h)) * scale).astype(BF16)
        key_grad = (dot(score_grad, head(query, h), 0, 0) * scale).astype(BF16)
        value_grad = dot(weights.astype(BF16), grad_h, 0, 0).astype(BF16)
        for at, (grad, w_ref) in enumerate(
            ((query_grad, wq_ref), (key_grad, wk_ref), (value_grad, wv_ref))
        ):
            grads[at * own + lo : at * own + lo + DH] = dot(grad, normed_one, 0, 0).astype(BF16)
            one_grad += dot(grad, w_ref[:, lo : lo + DH], 1, 1)
        diagonal = pltpu.roll(dot(score_grad, flip), 0, 1, stride=1, stride_axis=0)
        small2[h : h + 1] = jnp.sum(diagonal, axis=0, keepdims=True)

    chunk = grads_in.shape[1]
    owners = width // chunk

    def block(ref, index):
        return ref.at[pl.ds(pl.multiple_of(index * chunk, 16), chunk)]

    def guarded(condition, action):
        if owners == n_dp:
            action()
        else:
            pl.when(condition)(action)

    def scatter_copy(k, peer):
        return pltpu.make_async_remote_copy(
            src_ref=block(grads, peer),
            dst_ref=grads_in.at[me_d],
            send_sem=d_send.at[3, k],
            recv_sem=d_recv.at[3, k],
            device_id=(peer, me_t),
            device_id_type=MESH,
        )

    def scatter_start(k, carry):
        peer = lax.rem(me_d + k, n_dp)
        guarded(peer < owners, lambda: scatter_copy(k, peer).start())
        return carry

    lax.fori_loop(1, n_dp, scatter_start, 0)

    normal_one = x_full * inv_one
    row_sum = jnp.sum(one_grad * gain1 * normal_one, axis=1, keepdims=True)
    row2_part[...] = jnp.broadcast_to(to_row(row_sum), (8, rows))
    row2_in[me_t] = row2_part[...]
    for q in range(n_t):
        one_send[q] = one_grad[:, q * quarter : (q + 1) * quarter].astype(BF16)
    one_in[me_t] = one_send[me_t]
    eighth = over_tensor(7, lambda p: one_send.at[p], one_in.at[me_t])
    eighth += over_tensor(8, lambda p: row2_part, row2_in.at[me_t])
    finish(eighth)
    row_total = row2_in[0]
    one_part = one_in[0].astype(F32)
    for q in range(1, n_t):
        row_total += row2_in[q]
        one_part += one_in[q].astype(F32)
    row_mean = to_column(row_total[0:1]) / width
    normal_part = x_ref[...].astype(F32) * inv_one
    scaled_part = one_part * gain1_ref[...].astype(F32)
    dx_ref[...] = quarters[me_t] + inv_one * (scaled_part - normal_part * row_mean)
    gain_row = jnp.sum(one_part * normal_part, axis=0, keepdims=True)
    small2[head_count : head_count + 1, 0:quarter] = gain_row
    small2_in[me_d] = small2[...]
    small_two = (4, lambda p: small2, small2_in.at[me_d])
    dp_start(*small_two)

    def scatter_wait(k, carry):
        peer = lax.rem(me_d + k, n_dp)
        guarded(peer < owners, lambda: scatter_copy(k, peer).wait_send())
        guarded(me_d < owners, lambda: scatter_copy(k, peer).wait_recv())
        return carry

    lax.fori_loop(1, n_dp, scatter_wait, 0)

    def own_sum():
        grads_in[me_d] = block(grads, me_d)[...]
        total = grads_in[0].astype(F32)
        for d in range(1, n_dp):
            total += grads_in[d].astype(F32)
        block(grads_all, me_d)[...] = total.astype(BF16)

    guarded(me_d < owners, own_sum)

    def gather_copy(k, peer):
        return pltpu.make_async_remote_copy(
            src_ref=block(grads_all, me_d),
            dst_ref=block(grads_all, me_d),
            send_sem=d_send.at[5, k],
            recv_sem=d_recv.at[5, k],
            device_id=(peer, me_t),
            device_id_type=MESH,
        )

    def gather_start(k, carry):
        peer = lax.rem(me_d + k, n_dp)
        guarded(me_d < owners, lambda: gather_copy(k, peer).start())
        return carry

    lax.fori_loop(1, n_dp, gather_start, 0)

    dp_wait(*small_one)
    dp_wait(*small_two)
    small = small1_in[0].astype(F32)
    other = small2_in[0]
    for d in range(1, n_dp):
        small += small1_in[d].astype(F32)
        other += small2_in[d]
    dgain2_ref[...] = small[0:1]
    dwr_ref[...] = small[8 : 8 + n_dp]
    dgain1_ref[...] = other[head_count : head_count + 1, 0:quarter]
    for h in range(head_count):
        dtable_ref[:, h : h + 1] = jnp.sum(
            bucket_hot * other[h : h + 1], axis=1, keepdims=True
        )

    def gather_wait(k, carry):
        peer = lax.rem(me_d + k, n_dp)
        source = lax.rem(me_d + n_dp - k, n_dp)
        guarded(me_d < owners, lambda: gather_copy(k, peer).wait_send())

        def arrive():
            pltpu.make_async_remote_copy(
                src_ref=block(grads_all, source),
                dst_ref=block(grads_all, source),
                send_sem=d_send.at[5, k],
                recv_sem=d_recv.at[5, k],
                device_id=(peer, me_t),
                device_id_type=MESH,
            ).wait_recv()

        guarded(source < owners, arrive)
        return carry

    lax.fori_loop(1, n_dp, gather_wait, 0)
    for at, ref in enumerate((dwq_ref, dwk_ref, dwv_ref)):
        ref[...] = jnp.transpose(grads_all[at * own : (at + 1) * own].astype(F32))
    dwo_ref[...] = grads_all[3 * own :].astype(F32)


def on_device(
    activations, output_grad, seq_lengths, routes, buckets, norm1_gain, w_query, w_key, w_value,
    w_output, bias_table, norm2_gain, w_router, w_in, w_out,
):
    rows, quarter = activations.shape
    n_t = lax.axis_size("tensor")
    n_dp = lax.axis_size("dp")
    width = quarter * n_t
    own = w_query.shape[1]
    heads = own // DH
    slots = max(2, 9 * rows // (8 * n_dp))
    pad = -(-slots // 16) * 16
    chunk = max(16, width // n_dp)
    inner = w_in.shape[2]
    small_rows = -(-(8 + n_dp) // 16) * 16
    vmem = pl.BlockSpec(memory_space=pltpu.VMEM)
    smem = pl.BlockSpec(memory_space=pltpu.SMEM)

    def out(shape, dtype=F32):
        return jax.ShapeDtypeStruct(shape, dtype)

    results = pl.pallas_call(
        functools.partial(kernel, n_dp, n_t, slots, pad),
        out_shape=(
            out((rows, quarter), BF16),
            out((rows, quarter)),
            out((1, quarter)),
            out((width, own)),
            out((width, own)),
            out((width, own)),
            out((own, width)),
            out((bias_table.shape[0], heads)),
            out((1, width)),
            out((n_dp, width)),
            out((1, width, inner)),
            out((1, inner, width)),
        ),
        in_specs=[smem] + [vmem] * 14,
        out_specs=(vmem,) * 12,
        scratch_shapes=[
            pltpu.VMEM((n_t, 2, rows, quarter), BF16),
            pltpu.VMEM((n_t, 16, quarter), BF16),
            pltpu.VMEM((n_t, rows // n_t, width), BF16),
            pltpu.VMEM((n_t, rows // n_t, width), BF16),
            pltpu.VMEM((n_t, rows // n_t, width), BF16),
            pltpu.VMEM((n_dp, 2, pad, width), BF16),
            pltpu.VMEM((n_dp, 2, pad, width), BF16),
            pltpu.VMEM((n_t, 2, n_dp * pad, quarter), BF16),
            pltpu.VMEM((n_t, 2, n_dp * pad, quarter), BF16),
            pltpu.VMEM((n_dp, 2, pad, quarter), BF16),
            pltpu.VMEM((n_dp, 2, pad, quarter), BF16),
            pltpu.VMEM((n_t, rows, quarter), BF16),
            pltpu.VMEM((8, rows), F32),
            pltpu.VMEM((n_t, 8, rows), F32),
            pltpu.VMEM((n_t, rows, quarter), BF16),
            pltpu.VMEM((n_t, rows, quarter), BF16),
            pltpu.VMEM((8, rows), F32),
            pltpu.VMEM((n_t, 8, rows), F32),
            pltpu.VMEM((width, width), BF16),
            pltpu.VMEM((n_dp, chunk, width), BF16),
            pltpu.VMEM((width, width), BF16),
            pltpu.VMEM((small_rows, width), BF16),
            pltpu.VMEM((8, rows), F32),
            pltpu.VMEM((n_dp, small_rows, width), BF16),
            pltpu.VMEM((n_dp, 8, rows), F32),
            pltpu.VMEM((n_t, rows, quarter), F32),
            pltpu.VMEM((heads, rows, rows), F32),
            pltpu.VMEM((n_dp * pad, inner), BF16),
            pltpu.VMEM((n_dp * pad, inner), BF16),
            pltpu.SemaphoreType.DMA((9, n_t)),
            pltpu.SemaphoreType.DMA((9, n_t)),
            pltpu.SemaphoreType.DMA((6, n_dp)),
            pltpu.SemaphoreType.DMA((6, n_dp)),
            pltpu.SemaphoreType.DMA,
        ],
        compiler_params=pltpu.CompilerParams(
            collective_id=0, has_side_effects=True, vmem_limit_bytes=60 * 1024 * 1024
        ),
    )(
        seq_lengths, activations, output_grad, routes, buckets.reshape(1, rows),
        norm1_gain.reshape(1, quarter), w_query, w_key, w_value, w_output, bias_table,
        norm2_gain.reshape(1, width), w_router, w_in, w_out,
    )
    r = list(results)
    r[2] = r[2].reshape(quarter)
    r[8] = r[8].reshape(width)
    r[9] = jnp.transpose(r[9])
    return tuple(r)


def solution(mesh):
    in_specs = (
        P("dp", "tensor"),
        P("dp", "tensor"),
        P("dp"),
        P("dp", None),
        P(),
        P("tensor"),
        P(None, "tensor"),
        P(None, "tensor"),
        P(None, "tensor"),
        P("tensor", None),
        P(None, "tensor"),
        P(),
        P(),
        P("dp", None, "tensor"),
        P("dp", "tensor", None),
    )
    out_specs = (
        P("dp", "tensor"),
        P("dp", "tensor"),
        P("tensor"),
        P(None, "tensor"),
        P(None, "tensor"),
        P(None, "tensor"),
        P("tensor", None),
        P(None, "tensor"),
        P(),
        P(),
        P("dp", None, "tensor"),
        P("dp", "tensor", None),
    )
    return jax.shard_map(
        on_device, mesh=mesh, in_specs=in_specs, out_specs=out_specs, check_vma=False
    )
```

time: 395 us -> 199 us (0.50)
  waiting for transfers between devices: 179 us -> 0 us
  Pallas kernels: 0 us -> 163 us
  blocking collectives: 65 us -> 0 us
  matrix products: 30 us -> 0 us
  local copies, waits for them, and re-layouts: 57.6 us -> 32.3 us
  starting transfers between devices: 25 us -> 0 us
  other arithmetic: 17.7 us -> 1.29 us
  between operations: 16.7 us -> 0.68 us
    pallas_call x0 -> x1, Pallas kernels: none -> 163 us  [on_device(): pl.pallas_call(functools.partial(kernel, n_dp, n_t, slots, pad), out_shap...]
    psum x3 -> x0, waiting for transfers between devices: 135 us -> none  [the longest x1 73.9 us: on_device(): lax.psum((one_gain_grad, query_w_grad, key_w_grad, value_w_grad, output_w...]
    psum x2 -> x0, blocking collectives: 38.7 us -> none  [the longest x1 31.9 us: on_device(): lax.psum((one_gain_grad, query_w_grad, key_w_grad, value_w_grad, output_w...]
    dot_general x29 -> x0, matrix products: 30 us -> none  [the longest x14 20.4 us: contract(): lax.dot_general(left, right, (((left_axis,), (right_axis,)), ((), ())), p...]
    unnamed x7 -> x0, waiting for transfers between devices: 27 us -> none
    all_to_all x4 -> x0, starting transfers between devices: 24.7 us -> none  [the longest x2 12.5 us: to_experts(): return lax.all_to_all(values, 'dp', split_axis=0, concat_axis=0, tiled=True)]
    all_gather x3 -> x0, blocking collectives: 19.9 us -> none  [the longest x1 6.87 us: on_device(): lax.all_gather(token_part, 'tensor', axis=1, tiled=True).astype(jnp.float32)]
    all_to_all x4 -> x0, waiting for transfers between devices: 17.2 us -> none  [the longest x2 9.71 us: from_experts(): return lax.all_to_all(values, 'dp', split_axis=0, concat_axis=0, tiled=True)]
  transfers between devices with their start and end apart: 9 -> 0, of which waited for: 8 -> 0; matrix products, arithmetic and copies ran while one was open for 9% -> 0% of each run, Pallas kernels for 0% -> 0%
where the time goes in v1:
time: 199 us; the launch traced here: 197 us
  Pallas kernels  163 us (82%)
  local copies, waits for them, and re-layouts  32.3 us (16%)
    pallas_call x1, Pallas kernels, on_device(): pl.pallas_call(functools.partial(kernel, n_dp, n_t, slots, pad), out_shap...  163 us
    unnamed x31, local copies, waits for them, and re-layouts  29.8 us

profile of v1, /device:TPU:14, one launch (start us, length us, event | category | flops | bytes accessed | tf_op | source)
XLA Modules:
  0.0 197.4 jit_solution(2015509692138151786)
XLA Ops:
  0.6 0.0 copy-start.3
  0.7 1.3 reshape.40.gain1_ref
  1.9 1.3 reshape.41.gain2_ref
  3.2 1.4 copy.33.table_ref
  4.5 1.7 copy.27.x_ref
  6.2 1.7 copy.28.dy_ref
  7.8 1.5 copy.29.routes_ref
  9.3 1.5 copy.34.wr_ref
  10.8 1.9 copy.30.wq_ref
  12.7 1.9 copy.31.wk_ref
  14.6 0.0 copy-done.3
  14.6 0.9 copy.32.wv_ref
  15.5 163.1 %shard_map.238 = (bf16[256,192]{1,0:T(8,128)(2,1)}, f32[256,192]{1,0:T(8,128)}, f32[1,192]{1,0:T(1,128)}, f32[768,192]{1,0:T(8,128)}, f32[768,192]{1,0:T(8,128)}...) custom-call(s32[2]{0:T(128)} %lens_ref.1, ...), custom_call_target="tpu_custom_call" | custom-call | tf_op jit(solution)/shard_map/pallas_call | solution.py:440
  178.6 0.0 copy-start.2
  178.6 1.7 copy.35
  180.3 0.0 copy-start.5
  180.3 1.4 copy.40
  181.7 1.3 reduce
  183.0 1.7 copy.36
  184.7 0.0 copy-start.4
  184.7 0.0 copy-start.1
  184.7 2.3 %copy.37 = f32[768,192]{0,1:T(8,128)} copy(f32[768,192]{1,0:T(8,128)} %get-tuple-element.39) | data formatting | bytes 1179648
  187.1 2.2 %copy.38 = f32[768,192]{0,1:T(8,128)} copy(f32[768,192]{1,0:T(8,128)} %get-tuple-element.40) | data formatting | bytes 1179648
  189.3 0.0 copy-done.2
  189.3 1.1 copy.39
  190.4 0.0 copy-done.5
  190.4 0.6 copy.46
  190.9 1.9 copy.47
  192.8 0.0 copy-done.4
  192.8 0.6 copy.48
  193.4 0.0 copy-done.1
  193.4 0.0 copy-start
  193.5 1.4 copy.49
  194.9 1.1 copy-done
  196.0 1.4 copy.50
Async XLA Ops:
  0.6 14.0 %copy-start.3 = (bf16[768,192]{0,1:T(8,128)(2,1)S(1)}, bf16[768,192]{0,1:T(8,128)(2,1)}, u32[]{:S(2)}) copy-start(bf16[768,192]{0,1:T(8,128)(2,1)} %param.23) | copy-start | bytes 884740
  178.6 10.7 %copy-start.2 = (f32[768,192]{1,0:T(8,128)S(1)}, f32[768,192]{1,0:T(8,128)}, u32[]{:S(2)}) copy-start(f32[768,192]{1,0:T(8,128)} %get-tuple-element.41) | copy-start | bytes 1769476
  180.3 10.0 %copy-start.5 = (f32[1,192]{1,0:T(1,128)S(1)}, f32[1,192]{1,0:T(1,128)}, u32[]{:S(2)}) copy-start(f32[1,192]{1,0:T(1,128)} %get-tuple-element.26) | copy-start | bytes 2308
  184.7 8.1 %copy-start.4 = (f32[8,768]{1,0:T(8,128)S(1)}, f32[8,768]{1,0:T(8,128)}, u32[]{:S(2)}) copy-start(f32[8,768]{1,0:T(8,128)} %get-tuple-element.33) | copy-start | bytes 73732
  184.7 8.7 %copy-start.1 = (f32[1,768,768]{2,1,0:T(8,128)S(1)}, f32[1,768,768]{2,1,0:T(8,128)}, u32[]{:S(2)}) copy-start(f32[1,768,768]{2,1,0:T(8,128)} %get-tuple-element.70) | copy-start | bytes 7077892
  193.4 2.5 %copy-start = (f32[1,768,768]{2,1,0:T(8,128)S(1)}, f32[1,768,768]{2,1,0:T(8,128)}, u32[]{:S(2)}) copy-start(f32[1,768,768]{2,1,0:T(8,128)} %get-tuple-element.71) | copy-start | bytes 7077892

commit v2 on v1

v2 whole, which is shorter than its diff:
```python
import functools
import math

import jax
import jax.numpy as jnp
from jax import lax
from jax.experimental import pallas as pl
from jax.experimental.pallas import tpu as pltpu
from jax.sharding import PartitionSpec as P

DH = 64
EPSILON = 1e-06
NEGATIVE = -1e30
F32 = jnp.float32
BF16 = jnp.bfloat16
MESH = pl.DeviceIdType.MESH


def dot(left, right, left_axis=1, right_axis=0):
    return lax.dot_general(
        left, right, (((left_axis,), (right_axis,)), ((), ())), preferred_element_type=F32
    )


def iota(shape, axis):
    return lax.broadcasted_iota(jnp.int32, shape, axis)


def kernel(
    n_dp, n_t, slots, pad,
    lens_ref, x_ref, dy_ref, routes_ref, buckets_ref, gain1_ref, wq_ref, wk_ref, wv_ref, wo_ref,
    table_ref, gain2_ref, wr_ref, win_ref, wout_ref,
    out_ref, dx_ref, dgain1_ref, dwq_ref, dwk_ref, dwv_ref, dwo_ref, dtable_ref, dgain2_ref,
    dwr_ref, dwin_ref, dwout_ref,
    xs, gs, a_send, a_recv, a_sum, sent, arrived, parts, parts_in, back, back_in,
    eg_all, row_part, row_in, one_send, one_in, row2_part, row2_in,
    grads, pair_in, pair_sum, grads_in, grads_all, small1, small2, small1_in, small2_in,
    quarters, p_ref, activated, pre_grad,
    t_send, t_recv, d_send, d_recv, p_send, p_recv, z_send, z_recv, g_send, g_recv, f_send,
):
    me_d = lax.axis_index("dp")
    me_t = lax.axis_index("tensor")
    quarter, rows = x_ref.shape
    width = quarter * n_t
    head_count = wq_ref.shape[0] // DH
    scale = DH ** (-0.5)
    bucket_count = table_ref.shape[1]
    total_slots = n_dp * pad

    barrier = pltpu.get_barrier_semaphore()
    for k in range(1, n_t):
        pl.semaphore_signal(
            barrier, inc=1, device_id=(me_d, lax.rem(me_t + k, n_t)), device_id_type=MESH
        )

    def greet(k, carry):
        pl.semaphore_signal(
            barrier, inc=1, device_id=(lax.rem(me_d + k, n_dp), me_t), device_id_type=MESH
        )
        return carry

    lax.fori_loop(1, n_dp, greet, 0)
    pl.semaphore_wait(barrier, n_t - 1 + n_dp - 1)

    def over_tensor(phase, source, target):
        copies = []
        for k in range(1, n_t):
            peer = lax.rem(me_t + k, n_t)
            copy = pltpu.make_async_remote_copy(
                src_ref=source(peer),
                dst_ref=target,
                send_sem=t_send.at[phase, k],
                recv_sem=t_recv.at[phase, k],
                device_id=(me_d, peer),
                device_id_type=MESH,
            )
            copy.start()
            copies.append(copy)
        return copies

    def finish(copies):
        for copy in copies:
            copy.wait()

    def dp_copy(phase, k, source, target, peer):
        return pltpu.make_async_remote_copy(
            src_ref=source(peer),
            dst_ref=target,
            send_sem=d_send.at[phase, k],
            recv_sem=d_recv.at[phase, k],
            device_id=(peer, me_t),
            device_id_type=MESH,
        )

    def dp_start(phase, source, target):
        def body(k, carry):
            dp_copy(phase, k, source, target, lax.rem(me_d + k, n_dp)).start()
            return carry

        lax.fori_loop(1, n_dp, body, 0)

    def dp_wait(phase, source, target):
        def body(k, carry):
            dp_copy(phase, k, source, target, lax.rem(me_d + k, n_dp)).wait()
            return carry

        lax.fori_loop(1, n_dp, body, 0)

    xs[me_t, 0] = x_ref[...]
    xs[me_t, 1] = dy_ref[...]
    gs[me_t] = jnp.broadcast_to(gain1_ref[...].astype(F32), (16, quarter)).astype(BF16)
    first = over_tensor(0, lambda p: xs.at[me_t], xs.at[me_t])
    first += over_tensor(1, lambda p: gs.at[me_t], gs.at[me_t])

    first_len = lens_ref[0]
    both_len = first_len + lens_ref[1]
    row_col = iota((rows, 1), 0)
    row_row = iota((1, rows), 1)

    def segment_of(position):
        return jnp.where(position < first_len, 0, jnp.where(position < both_len, 1, 2))

    live = (row_col < both_len).astype(F32)
    at_i = iota((rows, rows), 0)
    at_j = iota((rows, rows), 1)
    allowed = (at_i >= at_j) & (segment_of(row_col) == segment_of(row_row))
    eye = at_i == at_j
    flip = (lax.rem(at_i + at_j, rows) == 0).astype(F32).astype(BF16)
    live_row = (row_row < both_len).astype(F32)

    def to_row(column):
        return jnp.sum(jnp.where(eye, column, 0.0), axis=0, keepdims=True)

    def to_column(line):
        return jnp.sum(jnp.where(eye, line, 0.0), axis=1, keepdims=True)

    routes = to_column(routes_ref[...].astype(F32))
    chosen = (routes.astype(jnp.int32) == iota((rows, n_dp), 1)).astype(F32)
    picked = chosen * live
    earlier = dot((at_j < at_i).astype(F32).astype(BF16), picked.astype(BF16))
    rank = jnp.sum(picked * earlier, axis=1, keepdims=True)
    slot = routes * pad + rank
    slot = jnp.where(live > 0, slot, -1.0)
    unpack = (slot == iota((rows, total_slots), 1).astype(F32)).astype(F32).astype(BF16)
    bucket_hot = (iota((bucket_count, rows), 0) == buckets_ref[...]).astype(F32)
    offset_bias = dot(table_ref[...], dot(bucket_hot.astype(BF16), flip).astype(BF16))

    finish(first)
    x_full = jnp.transpose(xs[:, 0].reshape(width, rows).astype(F32))
    dy_full = jnp.transpose(xs[:, 1].reshape(width, rows).astype(F32))
    gain1 = jnp.concatenate([gs[q].astype(F32)[0:1] for q in range(n_t)], axis=1)
    inv_one = lax.rsqrt(jnp.mean(x_full * x_full, axis=1, keepdims=True) + EPSILON)
    normed_one = (x_full * inv_one * gain1).astype(BF16)
    query = dot(normed_one, wq_ref[...], 1, 1).astype(BF16)
    key = dot(normed_one, wk_ref[...], 1, 1).astype(BF16)
    value = dot(normed_one, wv_ref[...], 1, 1).astype(BF16)

    def head(values, h):
        return values[:, h * DH : (h + 1) * DH]

    outs = []
    attn_part = jnp.zeros((rows, width), F32)
    for h in range(head_count):
        bias = jnp.broadcast_to(offset_bias[h : h + 1], (rows, rows))
        bias = pltpu.roll(bias, 0, 1, stride=1, stride_axis=0)
        scores = dot(head(query, h), head(key, h), 1, 1) * scale + bias
        scores = jnp.where(allowed, scores, NEGATIVE)
        weights = jnp.exp(scores - jnp.max(scores, axis=1, keepdims=True))
        weights = weights / jnp.sum(weights, axis=1, keepdims=True)
        p_ref[h] = weights
        outs.append(dot(weights.astype(BF16), head(value, h)).astype(BF16))
        attn_part += dot(outs[h], wo_ref[h * DH : (h + 1) * DH])

    share = rows // n_t
    a_send[...] = attn_part.astype(BF16).reshape(n_t, share, width)
    a_recv[me_t] = a_send[me_t]
    finish(over_tensor(2, lambda p: a_send.at[p], a_recv.at[me_t]))
    a_total = a_recv[0].astype(F32)
    for q in range(1, n_t):
        a_total += a_recv[q].astype(F32)
    a_sum[me_t] = a_total.astype(BF16)
    finish(over_tensor(3, lambda p: a_sum.at[me_t], a_sum.at[me_t]))
    hidden = x_full + live * a_sum[...].reshape(rows, width).astype(F32)
    inv_two = lax.rsqrt(jnp.mean(hidden * hidden, axis=1, keepdims=True) + EPSILON)
    gain2 = gain2_ref[...].astype(F32)
    normal_two = hidden * inv_two
    normed_two = (normal_two * gain2).astype(BF16)
    logits = dot(normed_two, wr_ref[...], 1, 1)
    probs = jnp.exp(logits - jnp.max(logits, axis=1, keepdims=True))
    probs = probs / jnp.sum(probs, axis=1, keepdims=True)
    gate = jnp.sum(probs * chosen, axis=1, keepdims=True)
    moe_grad = (live * gate * dy_full).astype(BF16)

    sent[:, 0] = dot(unpack, normed_two, 0, 0).astype(BF16).reshape(n_dp, pad, width)
    sent[:, 1] = dot(unpack, moe_grad, 0, 0).astype(BF16).reshape(n_dp, pad, width)
    arrived[me_d] = sent[me_d]
    dispatch = (0, lambda p: sent.at[p], arrived.at[me_d])
    dp_start(*dispatch)
    quarters[...] = jnp.transpose(hidden).reshape(n_t, quarter, rows)
    dp_wait(*dispatch)
    root = math.sqrt(2.0 / math.pi)
    step = total_slots if total_slots <= 512 else 256
    for begin in range(0, total_slots, step):
        span = slice(begin, begin + step)
        sources = slice(begin // pad, (begin + step) // pad)
        pre = dot(arrived[sources, 0].reshape(step, width), win_ref[0])
        square = pre * pre
        bent = jnp.tanh(root * (pre + 0.044715 * square * pre))
        activated[span] = (0.5 * pre * (1.0 + bent)).astype(BF16)
        slope = 0.5 * (1.0 + bent) + 0.5 * pre * (1.0 - bent * bent) * root * (
            1.0 + 3 * 0.044715 * square
        )
        wide = dot(wout_ref[0], activated[span], 0, 1).astype(BF16)
        parts[:, 0, :, span] = wide.reshape(n_t, quarter, step)
        act_grad = dot(arrived[sources, 1].reshape(step, width), wout_ref[0], 1, 1)
        pre_grad[span] = (act_grad * slope).astype(BF16)
        wide = dot(win_ref[0], pre_grad[span], 1, 1).astype(BF16)
        parts[:, 1, :, span] = wide.reshape(n_t, quarter, step)
    parts_in[me_t] = parts[me_t]
    shares = over_tensor(4, lambda p: parts.at[p], parts_in.at[me_t])
    dwout_ref[0] = dot(activated[...], arrived[:, 1].reshape(total_slots, width), 0, 0)
    dwin_ref[0] = dot(arrived[:, 0].reshape(total_slots, width), pre_grad[...], 0, 0)
    finish(shares)
    for s in range(2):
        total = parts_in[0, s].astype(F32)
        for q in range(1, n_t):
            total += parts_in[q, s].astype(F32)
        back[:, s] = jnp.transpose(total).astype(BF16).reshape(n_dp, pad, quarter)

    back_in[me_d] = back[me_d]
    home = (1, lambda p: back.at[p], back_in.at[me_d])
    dp_start(*home)
    dp_wait(*home)
    moe_quarter = dot(back_in[:, 0].reshape(total_slots, quarter), unpack, 0, 1)
    eg_all[me_t] = dot(back_in[:, 1].reshape(total_slots, quarter), unpack, 0, 1).astype(BF16)

    gate_part = jnp.sum(xs[me_t, 1].astype(F32) * moe_quarter, axis=0, keepdims=True)
    row_part[...] = jnp.broadcast_to(gate_part, (8, rows))
    row_in[me_t] = row_part[...]
    sixth = over_tensor(5, lambda p: eg_all.at[me_t], eg_all.at[me_t])
    sixth += over_tensor(6, lambda p: row_part, row_in.at[me_t])
    out_ref[...] = (quarters[me_t] + live_row * to_row(gate) * moe_quarter).astype(BF16)
    finish(sixth)
    row_total = row_in[0]
    for q in range(1, n_t):
        row_total += row_in[q]
    gate_grad = live * to_column(row_total[0:1])
    expert_grad = jnp.transpose(eg_all[...].reshape(width, rows).astype(F32))
    logit_grad = (gate_grad * gate * (chosen - probs)).astype(BF16)
    two_grad = expert_grad + dot(logit_grad, wr_ref[...])
    small1[0:8] = jnp.broadcast_to(
        jnp.sum(two_grad * normal_two, axis=0, keepdims=True), (8, width)
    ).astype(BF16)
    small1[8 : 8 + n_dp] = dot(logit_grad, normed_two, 0, 0).astype(BF16)
    if 8 + n_dp < small1.shape[0]:
        small1[8 + n_dp :] = jnp.zeros((small1.shape[0] - 8 - n_dp, width), BF16)
    small1_in[me_d] = small1[...]
    small_one = (2, lambda p: small1, small1_in.at[me_d])
    dp_start(*small_one)
    scaled_two = two_grad * gain2
    hidden_grad = dy_full + inv_two * (
        scaled_two - normal_two * jnp.mean(scaled_two * normal_two, axis=1, keepdims=True)
    )
    attn_grad = (live * hidden_grad).astype(BF16)
    quarters[...] = jnp.transpose(hidden_grad).reshape(n_t, quarter, rows)
    heads_grad = dot(attn_grad, wo_ref[...], 1, 1).astype(BF16)

    own = head_count * DH
    chunk = grads_in.shape[1]
    pairs = pair_in.shape[0]
    outer = n_dp // 2
    in_pair = lax.rem(me_d, 2)
    pair = me_d // 2
    mate = me_d + 1 - 2 * in_pair

    def block(ref, index):
        return ref.at[pl.ds(pl.multiple_of(index * chunk, 16), chunk)]

    def guarded(condition, action):
        if pairs == outer:
            action()
        else:
            pl.when(condition)(action)

    def to(source, target, send, recv, peer):
        return pltpu.make_async_remote_copy(
            src_ref=source, dst_ref=target, send_sem=send, recv_sem=recv,
            device_id=(peer, me_t), device_id_type=MESH,
        )

    def pair_copy(z):
        return to(
            block(grads, 2 * z + 1 - in_pair), pair_in.at[z], p_send.at[z], p_recv.at[z], mate
        )

    def outer_copy(z):
        return to(
            pair_sum.at[z], grads_in.at[pair], z_send.at[z], z_recv.at[pair], 2 * z + in_pair
        )

    def matrix(m):
        return range(m * (pairs // 4), (m + 1) * (pairs // 4))

    def pairs_start(m):
        for z in matrix(m):
            pair_copy(z).start()

    def pairs_pass(m):
        for z in matrix(m):
            pair_copy(z).wait()
            mine = block(grads, 2 * z + in_pair)[...].astype(F32)
            pair_sum[z] = (mine + pair_in[z].astype(F32)).astype(BF16)
            pl.when(pair != z)(outer_copy(z).start)

    def spans(h):
        return slice(h * DH, (h + 1) * DH)

    for h in range(head_count):
        lo = 3 * own + h * DH
        grads[lo : lo + DH] = dot(outs[h], attn_grad, 0, 0).astype(BF16)
    pairs_start(3)
    one_grad = jnp.zeros((rows, width), F32)
    small2[...] = jnp.zeros(small2.shape, F32)
    score_grads = []
    for h in range(head_count):
        weights = p_ref[h]
        grad_h = head(heads_grad, h)
        value_grad = dot(weights.astype(BF16), grad_h, 0, 0).astype(BF16)
        lo = 2 * own + h * DH
        grads[lo : lo + DH] = dot(value_grad, normed_one, 0, 0).astype(BF16)
        one_grad += dot(value_grad, wv_ref[spans(h)])
    pairs_start(2)
    for h in range(head_count):
        weights = p_ref[h]
        weight_grad = dot(head(heads_grad, h), head(value, h), 1, 1)
        score_grad = (
            weights * (weight_grad - jnp.sum(weights * weight_grad, axis=1, keepdims=True))
        ).astype(BF16)
        score_grads.append(score_grad)
        key_grad = (dot(score_grad, head(query, h), 0, 0) * scale).astype(BF16)
        lo = own + h * DH
        grads[lo : lo + DH] = dot(key_grad, normed_one, 0, 0).astype(BF16)
        one_grad += dot(key_grad, wk_ref[spans(h)])
    pairs_start(1)
    pairs_pass(3)
    for h in range(head_count):
        query_grad = (dot(score_grads[h], head(key, h)) * scale).astype(BF16)
        lo = h * DH
        grads[lo : lo + DH] = dot(query_grad, normed_one, 0, 0).astype(BF16)
        one_grad += dot(query_grad, wq_ref[spans(h)])
    pairs_start(0)
    pairs_pass(2)
    for h in range(head_count):
        diagonal = pltpu.roll(dot(score_grads[h], flip), 0, 1, stride=1, stride_axis=0)
        small2[h : h + 1] = jnp.sum(diagonal, axis=0, keepdims=True)

    normal_one = x_full * inv_one
    row_sum = jnp.sum(one_grad * gain1 * normal_one, axis=1, keepdims=True)
    row2_part[...] = jnp.broadcast_to(to_row(row_sum), (8, rows))
    row2_in[me_t] = row2_part[...]
    one_send[...] = jnp.transpose(one_grad).astype(BF16).reshape(n_t, quarter, rows)
    one_in[me_t] = one_send[me_t]
    eighth = over_tensor(7, lambda p: one_send.at[p], one_in.at[me_t])
    eighth += over_tensor(8, lambda p: row2_part, row2_in.at[me_t])
    pairs_pass(1)
    pairs_pass(0)
    finish(eighth)
    row_total = row2_in[0]
    one_part = one_in[0].astype(F32)
    for q in range(1, n_t):
        row_total += row2_in[q]
        one_part += one_in[q].astype(F32)
    row_mean = row_total[0:1] / width
    inv_row = to_row(inv_one)
    eye_quarter = iota((quarter, quarter), 0) == iota((quarter, quarter), 1)
    normal_part = x_ref[...].astype(F32) * inv_row
    gain_column = jnp.sum(
        jnp.where(eye_quarter, gain1_ref[...].astype(F32), 0.0), axis=1, keepdims=True
    )
    scaled_part = one_part * gain_column
    dx_ref[...] = quarters[me_t] + inv_row * (scaled_part - normal_part * row_mean)
    gain_sum = jnp.sum(one_part * normal_part, axis=1, keepdims=True)
    gain_row = jnp.sum(jnp.where(eye_quarter, gain_sum, 0.0), axis=0, keepdims=True)
    small2[head_count : head_count + 1, 0:quarter] = gain_row
    small2_in[me_d] = small2[...]
    small_two = (4, lambda p: small2, small2_in.at[me_d])
    dp_start(*small_two)

    for z in range(pairs):
        pl.when(pair != z)(outer_copy(z).wait_send)

    def own_sum():
        for k in range(1, outer):
            z = lax.rem(pair + k, outer)
            to(pair_sum.at[0], grads_in.at[z], z_send.at[0], z_recv.at[z], mate).wait_recv()
        grads_in[pair] = pair_sum[pair]
        total = grads_in[0].astype(F32)
        for z in range(1, outer):
            total += grads_in[z].astype(F32)
        block(grads_all, me_d)[...] = total.astype(BF16)

    def pass_block(index, send, peer):
        here = block(grads_all, index)
        return to(here, here, send, g_recv.at[index], peer)

    def own_copies():
        copies = [pass_block(me_d, g_send.at[0], mate)]
        for k in range(1, outer):
            peer = 2 * lax.rem(pair + k, outer) + in_pair
            copies.append(pass_block(me_d, g_send.at[k], peer))
        return copies

    def own_start():
        own_sum()
        for copy in reversed(own_copies()):
            copy.start()

    guarded(pair < pairs, own_start)

    def onward(k):
        source = lax.rem(pair + outer - k, outer)
        return source, pass_block(2 * source + in_pair, f_send.at[k], mate)

    def go_on(copy):
        copy.wait_recv()
        copy.start()

    for k in range(1, outer):
        source, copy = onward(k)
        guarded(source < pairs, functools.partial(go_on, copy))

    dp_wait(*small_one)
    dp_wait(*small_two)
    small = small1_in[0].astype(F32)
    other = small2_in[0]
    for d in range(1, n_dp):
        small += small1_in[d].astype(F32)
        other += small2_in[d]
    dgain2_ref[...] = small[0:1]
    dwr_ref[...] = small[8 : 8 + n_dp]
    dgain1_ref[...] = other[head_count : head_count + 1, 0:quarter]
    for h in range(head_count):
        sums = jnp.sum(bucket_hot * other[h : h + 1], axis=1, keepdims=True)
        corner = iota((bucket_count, bucket_count), 0) == iota((bucket_count, bucket_count), 1)
        dtable_ref[h : h + 1] = jnp.sum(jnp.where(corner, sums, 0.0), axis=0, keepdims=True)

    for z in range(pairs):
        pass_block(2 * z + 1 - in_pair, g_send.at[0], mate).wait_recv()

    def own_wait():
        for copy in own_copies():
            copy.wait_send()

    guarded(pair < pairs, own_wait)
    for k in range(1, outer):
        source, copy = onward(k)
        guarded(source < pairs, copy.wait_send)
    for at, ref in enumerate((dwq_ref, dwk_ref, dwv_ref)):
        ref[...] = grads_all[at * own : (at + 1) * own].astype(F32)
    dwo_ref[...] = grads_all[3 * own :].astype(F32)


def on_device(
    activations, output_grad, seq_lengths, routes, buckets, norm1_gain, w_query, w_key, w_value,
    w_output, bias_table, norm2_gain, w_router, w_in, w_out,
):
    rows, quarter = activations.shape
    n_t = lax.axis_size("tensor")
    n_dp = lax.axis_size("dp")
    width = quarter * n_t
    own = w_query.shape[1]
    heads = own // DH
    slots = max(2, 9 * rows // (8 * n_dp))
    pad = -(-slots // 16) * 16
    chunk = max(16, width // n_dp)
    inner = w_in.shape[2]
    pairs = width // chunk // 2
    small_rows = -(-(8 + n_dp) // 16) * 16
    vmem = pl.BlockSpec(memory_space=pltpu.VMEM)
    smem = pl.BlockSpec(memory_space=pltpu.SMEM)

    def out(shape, dtype=F32):
        return jax.ShapeDtypeStruct(shape, dtype)

    results = pl.pallas_call(
        functools.partial(kernel, n_dp, n_t, slots, pad),
        out_shape=(
            out((quarter, rows), BF16),
            out((quarter, rows)),
            out((1, quarter)),
            out((own, width)),
            out((own, width)),
            out((own, width)),
            out((own, width)),
            out((heads, bias_table.shape[0])),
            out((1, width)),
            out((n_dp, width)),
            out((1, width, inner)),
            out((1, inner, width)),
        ),
        in_specs=[smem] + [vmem] * 14,
        out_specs=(vmem,) * 12,
        scratch_shapes=[
            pltpu.VMEM((n_t, 2, quarter, rows), BF16),
            pltpu.VMEM((n_t, 16, quarter), BF16),
            pltpu.VMEM((n_t, rows // n_t, width), BF16),
            pltpu.VMEM((n_t, rows // n_t, width), BF16),
            pltpu.VMEM((n_t, rows // n_t, width), BF16),
            pltpu.VMEM((n_dp, 2, pad, width), BF16),
            pltpu.VMEM((n_dp, 2, pad, width), BF16),
            pltpu.VMEM((n_t, 2, quarter, n_dp * pad), BF16),
            pltpu.VMEM((n_t, 2, quarter, n_dp * pad), BF16),
            pltpu.VMEM((n_dp, 2, pad, quarter), BF16),
            pltpu.VMEM((n_dp, 2, pad, quarter), BF16),
            pltpu.VMEM((n_t, quarter, rows), BF16),
            pltpu.VMEM((8, rows), F32),
            pltpu.VMEM((n_t, 8, rows), F32),
            pltpu.VMEM((n_t, quarter, rows), BF16),
            pltpu.VMEM((n_t, quarter, rows), BF16),
            pltpu.VMEM((8, rows), F32),
            pltpu.VMEM((n_t, 8, rows), F32),
            pltpu.VMEM((width, width), BF16),
            pltpu.VMEM((pairs, chunk, width), BF16),
            pltpu.VMEM((pairs, chunk, width), BF16),
            pltpu.VMEM((n_dp // 2, chunk, width), BF16),
            pltpu.VMEM((width, width), BF16),
            pltpu.VMEM((small_rows, width), BF16),
            pltpu.VMEM((8, rows), F32),
            pltpu.VMEM((n_dp, small_rows, width), BF16),
            pltpu.VMEM((n_dp, 8, rows), F32),
            pltpu.VMEM((n_t, quarter, rows), F32),
            pltpu.VMEM((heads, rows, rows), F32),
            pltpu.VMEM((n_dp * pad, inner), BF16),
            pltpu.VMEM((n_dp * pad, inner), BF16),
            pltpu.SemaphoreType.DMA((9, n_t)),
            pltpu.SemaphoreType.DMA((9, n_t)),
            pltpu.SemaphoreType.DMA((6, n_dp)),
            pltpu.SemaphoreType.DMA((6, n_dp)),
            pltpu.SemaphoreType.DMA((pairs,)),
            pltpu.SemaphoreType.DMA((pairs,)),
            pltpu.SemaphoreType.DMA((pairs,)),
            pltpu.SemaphoreType.DMA((n_dp // 2,)),
            pltpu.SemaphoreType.DMA((n_dp // 2,)),
            pltpu.SemaphoreType.DMA((n_dp,)),
            pltpu.SemaphoreType.DMA((n_dp // 2,)),
        ],
        compiler_params=pltpu.CompilerParams(
            collective_id=0, has_side_effects=True, vmem_limit_bytes=60 * 1024 * 1024
        ),
    )(
        seq_lengths, activations.T, output_grad.T, routes.reshape(1, rows),
        buckets.reshape(1, rows), norm1_gain.reshape(1, quarter), w_query.T, w_key.T, w_value.T,
        w_output, bias_table.T, norm2_gain.reshape(1, width), w_router.T, w_in, w_out,
    )
    r = list(results)
    r[2] = r[2].reshape(quarter)
    r[8] = r[8].reshape(width)
    for at in (0, 1, 3, 4, 5, 7, 9):
        r[at] = jnp.transpose(r[at])
    return tuple(r)


def solution(mesh):
    in_specs = (
        P("dp", "tensor"),
        P("dp", "tensor"),
        P("dp"),
        P("dp", None),
        P(),
        P("tensor"),
        P(None, "tensor"),
        P(None, "tensor"),
        P(None, "tensor"),
        P("tensor", None),
        P(None, "tensor"),
        P(),
        P(),
        P("dp", None, "tensor"),
        P("dp", "tensor", None),
    )
    out_specs = (
        P("dp", "tensor"),
        P("dp", "tensor"),
        P("tensor"),
        P(None, "tensor"),
        P(None, "tensor"),
        P(None, "tensor"),
        P("tensor", None),
        P(None, "tensor"),
        P(),
        P(),
        P("dp", None, "tensor"),
        P("dp", "tensor", None),
    )
    return jax.shard_map(
        on_device, mesh=mesh, in_specs=in_specs, out_specs=out_specs, check_vma=False
    )
```

time: 199 us -> 171 us (0.86)
  local copies, waits for them, and re-layouts: 32.3 us -> 17.6 us
  Pallas kernels: 163 us -> 151 us
    unnamed x31 -> x23, local copies, waits for them, and re-layouts: 29.8 us -> 15.1 us
    pallas_call x1, Pallas kernels: 163 us -> 151 us  [on_device(): pl.pallas_call(functools.partial(kernel, n_dp, n_t, slots, pad), out_shap...]
where the time goes in v2:
time: 171 us
  Pallas kernels  151 us (88%)
  local copies, waits for them, and re-layouts  17.6 us (10%)
    pallas_call x1, Pallas kernels, on_device(): pl.pallas_call(functools.partial(kernel, n_dp, n_t, slots, pad), out_shap...  151 us
    unnamed x23, local copies, waits for them, and re-layouts  15.1 us

profile of v2, /device:TPU:14, one launch (start us, length us, event | category | flops | bytes accessed | tf_op | source)
XLA Modules:
  0.0 170.8 jit_solution(13512671558770704120)
XLA Ops:
  0.6 1.3 reshape.45.gain2_ref
  1.9 1.2 reshape.44.gain1_ref
  3.1 151.1 %shard_map.238 = (bf16[192,256]{1,0:T(8,128)(2,1)}, f32[192,256]{1,0:T(8,128)}, f32[1,192]{1,0:T(1,128)}, f32[192,768]{1,0:T(8,128)}, f32[192,768]{1,0:T(8,128)}...) custom-call(s32[2]{0:T(128)} %lens_ref.1, ...), custom_call_target="tpu_custom_call" | custom-call | tf_op jit(solution)/shard_map/pallas_call | solution.py:485
  154.3 0.0 copy-start.3
  154.3 0.0 copy-start.2
  154.3 1.4 reduce
  155.7 1.5 copy.38
  157.2 1.6 copy.39
  158.8 1.2 copy.40
  160.0 0.0 copy-start.5
  160.0 0.0 copy-start.4
  160.0 0.0 copy-start.1
  160.0 2.1 %copy.41 = f32[768,192]{0,1:T(8,128)} copy(f32[768,192]{0,1:T(8,128)} %bitcast.19) | data formatting | bytes 1179648
  162.1 1.9 %copy.42 = f32[768,192]{0,1:T(8,128)} copy(f32[768,192]{0,1:T(8,128)} %bitcast.18) | data formatting | bytes 1179648
  164.0 0.0 copy-done.3
  164.0 0.8 copy.43
  164.8 0.0 copy-done.2
  164.8 0.8 copy.44
  165.6 0.0 copy-done.5
  165.6 0.6 copy.45
  166.2 0.0 copy-done.4
  166.2 0.6 copy.46
  166.8 0.0 copy-done.1
  166.8 0.0 copy-start
  166.8 1.4 copy.47
  168.2 1.1 copy-done
  169.3 1.4 copy.48
Async XLA Ops:
  154.3 9.7 %copy-start.3 = (f32[192,768]{1,0:T(8,128)S(1)}, f32[192,768]{1,0:T(8,128)}, u32[]{:S(2)}) copy-start(f32[192,768]{1,0:T(8,128)} %get-tuple-element.29) | copy-start | bytes 1769476
  154.3 10.5 %copy-start.2 = (f32[192,768]{1,0:T(8,128)S(1)}, f32[192,768]{1,0:T(8,128)}, u32[]{:S(2)}) copy-start(f32[192,768]{1,0:T(8,128)} %get-tuple-element.54) | copy-start | bytes 1769476
  160.0 5.6 %copy-start.5 = (f32[3,32]{1,0:T(4,128)S(1)}, f32[3,32]{1,0:T(4,128)}, u32[]{:S(2)}) copy-start(f32[3,32]{1,0:T(4,128)} %get-tuple-element.31) | copy-start | bytes 1156
  160.0 6.2 %copy-start.4 = (f32[8,768]{1,0:T(8,128)S(1)}, f32[8,768]{1,0:T(8,128)}, u32[]{:S(2)}) copy-start(f32[8,768]{1,0:T(8,128)} %get-tuple-element.33) | copy-start | bytes 73732
  160.0 6.8 %copy-start.1 = (f32[1,768,768]{2,1,0:T(8,128)S(1)}, f32[1,768,768]{2,1,0:T(8,128)}, u32[]{:S(2)}) copy-start(f32[1,768,768]{2,1,0:T(8,128)} %get-tuple-element.58) | copy-start | bytes 7077892
  166.8 2.5 %copy-start = (f32[1,768,768]{2,1,0:T(8,128)S(1)}, f32[1,768,768]{2,1,0:T(8,128)}, u32[]{:S(2)}) copy-start(f32[1,768,768]{2,1,0:T(8,128)} %get-tuple-element.59) | copy-start | bytes 7077892
